TPU v7x, 256 devices: a whole 4x4x8 slice. The times are simulated.
256 devices in a mesh: gx: 16 (over z, y_lo), gy: 16 (over y_hi, x, core).
Axes of the slice: x: 4, y: 4 (y_hi: 2, y_lo: 2; y = y_hi * 2 + y_lo), z: 8, core: 2. Of those that a mesh axis runs over, the one named last changes fastest.
Arguments:
- fields: float32 [6, 4096, 4096], P(None, 'gx', 'gy'), may hold values from -6 to 6
- inv_eps: float32 [4096, 4096], P('gx', 'gy'), may hold values from 0.75 to 1
- fwd_dft: float32 [3, 2, 3, 4096, 4096], P(None, None, None, 'gx', 'gy'), may hold values from -6 to 6
- phase_start: float32 [3], replicated, may hold values from -3.140625 to 3.140625
- omega: float32 [3], replicated, may hold values from 0.3 to 1.2
- mask: int32 [4096, 4096], P('gx', 'gy'), may hold values 0 or 1
Outputs:
- fields_out: float32 [6, 4096, 4096], P(None, 'gx', 'gy')
- gradient: float32 [4096, 4096], P('gx', 'gy')
All inputs are finite; a program needn't handle non-finite values. No bound on the sum of `mask` on one device may be relied on, other than what follows from the above.
Results may differ from a plain program's by a relative error of at most 0.000034.
Values sent between devices are 32-bit elements; how exact they have to be, the bound alone decides.
No kernel may reach another device: no remote copies, remote signals or barrier semaphores. Data moves between devices by JAX's collectives and lax.ppermute only.
A program may use at most 128 MiB of HBM per device.

v0:
```python
import jax
import jax.numpy as jnp
import numpy as np
from jax import lax
from jax.sharding import PartitionSpec as P

STEPS = 24
NF = 3
RADIUS = 3


courant = 0.68


def shifted(block, axis, distance):
    devices = range(lax.axis_size(axis))
    route = [((i - distance) % len(devices), i) for i in devices]
    return lax.ppermute(block, axis, route)


def padded_2(x, sides, width):
    for axis, dim in sides:
        count, length = (lax.axis_size(axis), x.shape[dim])
        up = [(i, (i + 1) % count) for i in range(count)]
        down = [(j, i) for i, j in up]
        last = lax.slice_in_dim(x, length - width, length, axis=dim)
        first = lax.slice_in_dim(x, 0, width, axis=dim)
        before = lax.ppermute(last, axis, up)
        after = lax.ppermute(first, axis, down)
        x = jnp.concatenate([before, x, after], axis=dim)
    return x


def filter_table(radius):
    offsets = np.arange(-radius, radius + 1)
    dist = np.sqrt(offsets[:, None] ** 2 + offsets[None, :] ** 2)
    table = np.maximum(0.0, radius - dist)
    return table / table.sum()


def update_h(ex, ey, ez, hx, hy, hz, ey_nx, ez_nx, ex_ny, ez_ny):
    hx = hx - courant * (ez_ny - ez)
    hy = hy + courant * (ez_nx - ez)
    hz = hz - courant * (ey_nx - ey - (ex_ny - ex))
    return (hx, hy, hz)


def update_e(ex, ey, ez, hx, hy, hz, inv_eps, hy_px, hz_px, hx_py, hz_py):
    factor = courant * inv_eps
    ex = ex + factor * (hz - hz_py)
    ey = ey - factor * (hz - hz_px)
    ez = ez + factor * (hy - hy_px - (hx - hx_py))
    return (ex, ey, ez)


def accumulate(acc, efield, count, phase_start, omega):
    theta = phase_start + omega * count.astype(jnp.float32)
    coefs = jnp.stack([jnp.cos(theta), jnp.sin(theta)], axis=1) / STEPS
    return acc + coefs[:, :, None, None, None] * efield[None, None]


def with_edge(plane, edge, dim, step):
    rolled = jnp.roll(plane, -step, dim)
    index = lax.broadcasted_iota(jnp.int32, plane.shape, dim)
    target = plane.shape[dim] - 1 if step > 0 else 0
    spread = edge[None, :] if dim == 0 else edge[:, None]
    return jnp.where(index == target, spread, rolled)


def local(fields, inv_eps, fwd_dft, phase_start, omega, mask):
    rows_x = fields.shape[1]
    rows_y = fields.shape[2]
    acc = jnp.zeros((NF, 2, 3, rows_x, rows_y), jnp.float32)

    def advance(count, carry):
        state, acc = carry
        ex, ey, ez, hx, hy, hz = [state[k] for k in range(6)]
        recv_x = shifted(jnp.stack([ey[0], ez[0]]), "gx", -1)
        recv_y = shifted(jnp.stack([ex[:, 0], ez[:, 0]]), "gy", -1)
        ey_nx = with_edge(ey, recv_x[0], 0, 1)
        ez_nx = with_edge(ez, recv_x[1], 0, 1)
        ex_ny = with_edge(ex, recv_y[0], 1, 1)
        ez_ny = with_edge(ez, recv_y[1], 1, 1)
        hx, hy, hz = update_h(ex, ey, ez, hx, hy, hz, ey_nx, ez_nx, ex_ny, ez_ny)
        back_x = shifted(jnp.stack([hy[-1], hz[-1]]), "gx", 1)
        back_y = shifted(jnp.stack([hx[:, -1], hz[:, -1]]), "gy", 1)
        hy_px = with_edge(hy, back_x[0], 0, -1)
        hz_px = with_edge(hz, back_x[1], 0, -1)
        hx_py = with_edge(hx, back_y[0], 1, -1)
        hz_py = with_edge(hz, back_y[1], 1, -1)
        ex, ey, ez = update_e(ex, ey, ez, hx, hy, hz, inv_eps, hy_px, hz_px, hx_py, hz_py)
        acc = accumulate(acc, jnp.stack([ex, ey, ez]), count, phase_start, omega)
        return (jnp.stack([ex, ey, ez, hx, hy, hz]), acc)

    state, acc = lax.fori_loop(0, STEPS, advance, (fields, acc))
    prod = acc[:, 0] * fwd_dft[:, 0] - acc[:, 1] * fwd_dft[:, 1]
    raw = jnp.sum(prod, axis=(0, 1)) * mask.astype(jnp.float32)
    padded = padded_2(raw, (("gx", 0), ("gy", 1)), RADIUS)
    table = filter_table(RADIUS)
    gradient = jnp.zeros_like(raw)
    for ia in range(2 * RADIUS + 1):
        for ib in range(2 * RADIUS + 1):
            weight = float(table[ia, ib])
            if weight > 0.0:
                gradient = gradient + weight * padded[ia : ia + rows_x, ib : ib + rows_y]
    return (state, gradient)


def solution(mesh):
    return jax.shard_map(
        local,
        mesh=mesh,
        in_specs=(
            P(None, "gx", "gy"),
            P("gx", "gy"),
            P(None, None, None, "gx", "gy"),
            P(),
            P(),
            P("gx", "gy"),
        ),
        out_specs=(P(None, "gx", "gy"), P("gx", "gy")),
        check_vma=False,
    )
```

profile of v0, /device:TPU:16, one launch (start us, length us, event | category | flops | bytes accessed | tf_op | source)
XLA Modules:
  0.0 629.8 jit_solution(276183666902376739)
XLA Ops:
  2.1 606.2 %while.16 = (s32[]{:T(128)}, f32[6,256,256]{2,1,0:T(8,128)S(1)}, f32[3,2,3,256,256]{4,3,2,1,0:T(8,128)}, f32[256,256]{1,0:T(8,128)S(1)}, f32[3]{0:T(128)}, /*index=5*/f32[3]{0:T(128)}, s32[]{:T(128)}, s32[]{:T(128)}) while((s32[]{:T(128)}, f32[6,256,256]{2,1,0:T(8,128)S(1)}, f32[3,2,3,256,256]{4,3,2,1,0:T(8,128)}, ...), condition=%wide.region_1.2_spmd.clone, body=%wide.region_0.1_spmd.clone.sunk | while | flops 7866901 | bytes 69704232 | solution.py:95
  3.2 6.6 %collective-permute-start = (f32[2,256]{1,0:T(2,128)}, f32[2,256]{1,0:T(2,128)}, u32[]{:S(2)}, u32[]{:S(2)}) collective-permute-start(f32[2,256]{1,0:T(2,128)} %pad_maximum_fusion.14), channel_id=1, source_target_pairs={{16,0},{32,16},{48,32},{64,48},{80,64},{96,80},{112,96},{128,112},... | collective-permute-start | bytes 6152 | tf_op jit(solution)/shard_map/while/body/eval_jaxpr/ppermute | solution.py:18
  21.0 6.5 %collective-permute-done.2 = f32[2,256]{1,0:T(2,128)S(1)} collective-permute-done((f32[2,256]{1,0:T(2,128)S(1)}, f32[2,256]{1,0:T(2,128)S(1)}, u32[]{:S(2)}, u32[]{:S(2)}) %collective-permute-start.2) | collective-permute-done | bytes 2080 | tf_op jit(solution)/shard_map/while/body/eval_jaxpr/ppermute | solution.py:18
  45.9 2.2 collective-permute-start.3
  48.2 4.3 collective-permute-done.2
  70.9 2.2 collective-permute-start.3
  73.2 4.3 collective-permute-done.2
  95.9 2.2 collective-permute-start.3
  98.2 4.3 collective-permute-done.2
  120.9 2.2 collective-permute-start.3
  123.2 4.3 collective-permute-done.2
  145.9 2.2 collective-permute-start.3
  148.2 4.3 collective-permute-done.2
  170.9 2.2 collective-permute-start.3
  173.2 4.3 collective-permute-done.2
  195.9 2.2 collective-permute-start.3
  198.2 4.3 collective-permute-done.2
  220.9 2.2 collective-permute-start.3
  223.2 4.3 collective-permute-done.2
  245.9 2.2 collective-permute-start.3
  248.2 4.3 collective-permute-done.2
  270.9 2.2 collective-permute-start.3
  273.2 4.3 collective-permute-done.2
  295.9 2.2 collective-permute-start.3
  298.2 4.3 collective-permute-done.2
  320.9 2.2 collective-permute-start.3
  323.2 4.3 collective-permute-done.2
  345.9 2.2 collective-permute-start.3
  348.2 4.3 collective-permute-done.2
  370.9 2.2 collective-permute-start.3
  373.2 4.3 collective-permute-done.2
  395.9 2.2 collective-permute-start.3
  398.2 4.3 collective-permute-done.2
  420.9 2.2 collective-permute-start.3
  423.2 4.3 collective-permute-done.2
  445.9 2.2 collective-permute-start.3
  448.2 4.3 collective-permute-done.2
  473.2 4.3 collective-permute-done.2
  498.2 4.3 collective-permute-done.2
  520.9 2.2 collective-permute-start.3
  523.2 4.3 collective-permute-done.2
  548.2 4.3 collective-permute-done.2
  570.9 2.2 collective-permute-start.3
  573.2 4.3 collective-permute-done.2
  598.2 4.3 collective-permute-done.2
  608.3 5.0 subtract_reduce_fusion
  619.4 5.3 collective-permute-start.7
  624.8 2.7 collective-permute-done.6
  (1561 shorter events, 453.6 us)
Async XLA Ops:
  3.2 16.3 %collective-permute-start = (f32[2,256]{1,0:T(2,128)}, f32[2,256]{1,0:T(2,128)}, u32[]{:S(2)}, u32[]{:S(2)}) collective-permute-start(f32[2,256]{1,0:T(2,128)} %pad_maximum_fusion.14), channel_id=1, source_target_pairs={{16,0},{32,16},{48,32},{64,48},{80,64},{96,80},{112,96},{128,112},... | collective-permute-start | bytes 6152 | tf_op jit(solution)/shard_map/while/body/eval_jaxpr/ppermute | solution.py:18
  20.9 6.9 %collective-permute-start.3 = (f32[2,256]{1,0:T(2,128)S(1)}, f32[2,256]{1,0:T(2,128)S(1)}, u32[]{:S(2)}, u32[]{:S(2)}) collective-permute-start(f32[2,256]{1,0:T(2,128)S(1)} %pad_maximum_fusion.17), channel_id=1, source_target_pairs={{240,0},{0,16},{16,32},{32,48},{48,64},{64,80},{80,96},{96,112},{1... | collective-permute-start | bytes 6152 | tf_op jit(solution)/shard_map/while/body/eval_jaxpr/ppermute | solution.py:18
  34.5 10.1 %collective-permute-start = (f32[2,256]{1,0:T(2,128)}, f32[2,256]{1,0:T(2,128)}, u32[]{:S(2)}, u32[]{:S(2)}) collective-permute-start(f32[2,256]{1,0:T(2,128)} %pad_maximum_fusion.14), channel_id=1, source_target_pairs={{16,0},{32,16},{48,32},{64,48},{80,64},{96,80},{112,96},{128,112},... | collective-permute-start | bytes 6152 | tf_op jit(solution)/shard_map/while/body/eval_jaxpr/ppermute | solution.py:18
  45.9 6.9 %collective-permute-start.3 = (f32[2,256]{1,0:T(2,128)S(1)}, f32[2,256]{1,0:T(2,128)S(1)}, u32[]{:S(2)}, u32[]{:S(2)}) collective-permute-start(f32[2,256]{1,0:T(2,128)S(1)} %pad_maximum_fusion.17), channel_id=1, source_target_pairs={{240,0},{0,16},{16,32},{32,48},{48,64},{64,80},{80,96},{96,112},{1... | collective-permute-start | bytes 6152 | tf_op jit(solution)/shard_map/while/body/eval_jaxpr/ppermute | solution.py:18
  59.5 10.1 %collective-permute-start = (f32[2,256]{1,0:T(2,128)}, f32[2,256]{1,0:T(2,128)}, u32[]{:S(2)}, u32[]{:S(2)}) collective-permute-start(f32[2,256]{1,0:T(2,128)} %pad_maximum_fusion.14), channel_id=1, source_target_pairs={{16,0},{32,16},{48,32},{64,48},{80,64},{96,80},{112,96},{128,112},... | collective-permute-start | bytes 6152 | tf_op jit(solution)/shard_map/while/body/eval_jaxpr/ppermute | solution.py:18
  70.9 6.9 %collective-permute-start.3 = (f32[2,256]{1,0:T(2,128)S(1)}, f32[2,256]{1,0:T(2,128)S(1)}, u32[]{:S(2)}, u32[]{:S(2)}) collective-permute-start(f32[2,256]{1,0:T(2,128)S(1)} %pad_maximum_fusion.17), channel_id=1, source_target_pairs={{240,0},{0,16},{16,32},{32,48},{48,64},{64,80},{80,96},{96,112},{1... | collective-permute-start | bytes 6152 | tf_op jit(solution)/shard_map/while/body/eval_jaxpr/ppermute | solution.py:18
  84.5 10.1 %collective-permute-start = (f32[2,256]{1,0:T(2,128)}, f32[2,256]{1,0:T(2,128)}, u32[]{:S(2)}, u32[]{:S(2)}) collective-permute-start(f32[2,256]{1,0:T(2,128)} %pad_maximum_fusion.14), channel_id=1, source_target_pairs={{16,0},{32,16},{48,32},{64,48},{80,64},{96,80},{112,96},{128,112},... | collective-permute-start | bytes 6152 | tf_op jit(solution)/shard_map/while/body/eval_jaxpr/ppermute | solution.py:18
  95.9 6.9 %collective-permute-start.3 = (f32[2,256]{1,0:T(2,128)S(1)}, f32[2,256]{1,0:T(2,128)S(1)}, u32[]{:S(2)}, u32[]{:S(2)}) collective-permute-start(f32[2,256]{1,0:T(2,128)S(1)} %pad_maximum_fusion.17), channel_id=1, source_target_pairs={{240,0},{0,16},{16,32},{32,48},{48,64},{64,80},{80,96},{96,112},{1... | collective-permute-start | bytes 6152 | tf_op jit(solution)/shard_map/while/body/eval_jaxpr/ppermute | solution.py:18
  109.5 10.1 %collective-permute-start = (f32[2,256]{1,0:T(2,128)}, f32[2,256]{1,0:T(2,128)}, u32[]{:S(2)}, u32[]{:S(2)}) collective-permute-start(f32[2,256]{1,0:T(2,128)} %pad_maximum_fusion.14), channel_id=1, source_target_pairs={{16,0},{32,16},{48,32},{64,48},{80,64},{96,80},{112,96},{128,112},... | collective-permute-start | bytes 6152 | tf_op jit(solution)/shard_map/while/body/eval_jaxpr/ppermute | solution.py:18
  120.9 6.9 %collective-permute-start.3 = (f32[2,256]{1,0:T(2,128)S(1)}, f32[2,256]{1,0:T(2,128)S(1)}, u32[]{:S(2)}, u32[]{:S(2)}) collective-permute-start(f32[2,256]{1,0:T(2,128)S(1)} %pad_maximum_fusion.17), channel_id=1, source_target_pairs={{240,0},{0,16},{16,32},{32,48},{48,64},{64,80},{80,96},{96,112},{1... | collective-permute-start | bytes 6152 | tf_op jit(solution)/shard_map/while/body/eval_jaxpr/ppermute | solution.py:18
  134.5 10.1 %collective-permute-start = (f32[2,256]{1,0:T(2,128)}, f32[2,256]{1,0:T(2,128)}, u32[]{:S(2)}, u32[]{:S(2)}) collective-permute-start(f32[2,256]{1,0:T(2,128)} %pad_maximum_fusion.14), channel_id=1, source_target_pairs={{16,0},{32,16},{48,32},{64,48},{80,64},{96,80},{112,96},{128,112},... | collective-permute-start | bytes 6152 | tf_op jit(solution)/shard_map/while/body/eval_jaxpr/ppermute | solution.py:18
  145.9 6.9 %collective-permute-start.3 = (f32[2,256]{1,0:T(2,128)S(1)}, f32[2,256]{1,0:T(2,128)S(1)}, u32[]{:S(2)}, u32[]{:S(2)}) collective-permute-start(f32[2,256]{1,0:T(2,128)S(1)} %pad_maximum_fusion.17), channel_id=1, source_target_pairs={{240,0},{0,16},{16,32},{32,48},{48,64},{64,80},{80,96},{96,112},{1... | collective-permute-start | bytes 6152 | tf_op jit(solution)/shard_map/while/body/eval_jaxpr/ppermute | solution.py:18
  159.5 10.1 %collective-permute-start = (f32[2,256]{1,0:T(2,128)}, f32[2,256]{1,0:T(2,128)}, u32[]{:S(2)}, u32[]{:S(2)}) collective-permute-start(f32[2,256]{1,0:T(2,128)} %pad_maximum_fusion.14), channel_id=1, source_target_pairs={{16,0},{32,16},{48,32},{64,48},{80,64},{96,80},{112,96},{128,112},... | collective-permute-start | bytes 6152 | tf_op jit(solution)/shard_map/while/body/eval_jaxpr/ppermute | solution.py:18
  170.9 6.9 %collective-permute-start.3 = (f32[2,256]{1,0:T(2,128)S(1)}, f32[2,256]{1,0:T(2,128)S(1)}, u32[]{:S(2)}, u32[]{:S(2)}) collective-permute-start(f32[2,256]{1,0:T(2,128)S(1)} %pad_maximum_fusion.17), channel_id=1, source_target_pairs={{240,0},{0,16},{16,32},{32,48},{48,64},{64,80},{80,96},{96,112},{1... | collective-permute-start | bytes 6152 | tf_op jit(solution)/shard_map/while/body/eval_jaxpr/ppermute | solution.py:18
  184.5 10.1 %collective-permute-start = (f32[2,256]{1,0:T(2,128)}, f32[2,256]{1,0:T(2,128)}, u32[]{:S(2)}, u32[]{:S(2)}) collective-permute-start(f32[2,256]{1,0:T(2,128)} %pad_maximum_fusion.14), channel_id=1, source_target_pairs={{16,0},{32,16},{48,32},{64,48},{80,64},{96,80},{112,96},{128,112},... | collective-permute-start | bytes 6152 | tf_op jit(solution)/shard_map/while/body/eval_jaxpr/ppermute | solution.py:18
  195.9 6.9 %collective-permute-start.3 = (f32[2,256]{1,0:T(2,128)S(1)}, f32[2,256]{1,0:T(2,128)S(1)}, u32[]{:S(2)}, u32[]{:S(2)}) collective-permute-start(f32[2,256]{1,0:T(2,128)S(1)} %pad_maximum_fusion.17), channel_id=1, source_target_pairs={{240,0},{0,16},{16,32},{32,48},{48,64},{64,80},{80,96},{96,112},{1... | collective-permute-start | bytes 6152 | tf_op jit(solution)/shard_map/while/body/eval_jaxpr/ppermute | solution.py:18
  209.5 10.1 %collective-permute-start = (f32[2,256]{1,0:T(2,128)}, f32[2,256]{1,0:T(2,128)}, u32[]{:S(2)}, u32[]{:S(2)}) collective-permute-start(f32[2,256]{1,0:T(2,128)} %pad_maximum_fusion.14), channel_id=1, source_target_pairs={{16,0},{32,16},{48,32},{64,48},{80,64},{96,80},{112,96},{128,112},... | collective-permute-start | bytes 6152 | tf_op jit(solution)/shard_map/while/body/eval_jaxpr/ppermute | solution.py:18
  220.9 6.9 %collective-permute-start.3 = (f32[2,256]{1,0:T(2,128)S(1)}, f32[2,256]{1,0:T(2,128)S(1)}, u32[]{:S(2)}, u32[]{:S(2)}) collective-permute-start(f32[2,256]{1,0:T(2,128)S(1)} %pad_maximum_fusion.17), channel_id=1, source_target_pairs={{240,0},{0,16},{16,32},{32,48},{48,64},{64,80},{80,96},{96,112},{1... | collective-permute-start | bytes 6152 | tf_op jit(solution)/shard_map/while/body/eval_jaxpr/ppermute | solution.py:18
  234.5 10.1 %collective-permute-start = (f32[2,256]{1,0:T(2,128)}, f32[2,256]{1,0:T(2,128)}, u32[]{:S(2)}, u32[]{:S(2)}) collective-permute-start(f32[2,256]{1,0:T(2,128)} %pad_maximum_fusion.14), channel_id=1, source_target_pairs={{16,0},{32,16},{48,32},{64,48},{80,64},{96,80},{112,96},{128,112},... | collective-permute-start | bytes 6152 | tf_op jit(solution)/shard_map/while/body/eval_jaxpr/ppermute | solution.py:18
  245.9 6.9 %collective-permute-start.3 = (f32[2,256]{1,0:T(2,128)S(1)}, f32[2,256]{1,0:T(2,128)S(1)}, u32[]{:S(2)}, u32[]{:S(2)}) collective-permute-start(f32[2,256]{1,0:T(2,128)S(1)} %pad_maximum_fusion.17), channel_id=1, source_target_pairs={{240,0},{0,16},{16,32},{32,48},{48,64},{64,80},{80,96},{96,112},{1... | collective-permute-start | bytes 6152 | tf_op jit(solution)/shard_map/while/body/eval_jaxpr/ppermute | solution.py:18
  259.5 10.1 %collective-permute-start = (f32[2,256]{1,0:T(2,128)}, f32[2,256]{1,0:T(2,128)}, u32[]{:S(2)}, u32[]{:S(2)}) collective-permute-start(f32[2,256]{1,0:T(2,128)} %pad_maximum_fusion.14), channel_id=1, source_target_pairs={{16,0},{32,16},{48,32},{64,48},{80,64},{96,80},{112,96},{128,112},... | collective-permute-start | bytes 6152 | tf_op jit(solution)/shard_map/while/body/eval_jaxpr/ppermute | solution.py:18
  270.9 6.9 %collective-permute-start.3 = (f32[2,256]{1,0:T(2,128)S(1)}, f32[2,256]{1,0:T(2,128)S(1)}, u32[]{:S(2)}, u32[]{:S(2)}) collective-permute-start(f32[2,256]{1,0:T(2,128)S(1)} %pad_maximum_fusion.17), channel_id=1, source_target_pairs={{240,0},{0,16},{16,32},{32,48},{48,64},{64,80},{80,96},{96,112},{1... | collective-permute-start | bytes 6152 | tf_op jit(solution)/shard_map/while/body/eval_jaxpr/ppermute | solution.py:18
  284.5 10.1 %collective-permute-start = (f32[2,256]{1,0:T(2,128)}, f32[2,256]{1,0:T(2,128)}, u32[]{:S(2)}, u32[]{:S(2)}) collective-permute-start(f32[2,256]{1,0:T(2,128)} %pad_maximum_fusion.14), channel_id=1, source_target_pairs={{16,0},{32,16},{48,32},{64,48},{80,64},{96,80},{112,96},{128,112},... | collective-permute-start | bytes 6152 | tf_op jit(solution)/shard_map/while/body/eval_jaxpr/ppermute | solution.py:18
  295.9 6.9 %collective-permute-start.3 = (f32[2,256]{1,0:T(2,128)S(1)}, f32[2,256]{1,0:T(2,128)S(1)}, u32[]{:S(2)}, u32[]{:S(2)}) collective-permute-start(f32[2,256]{1,0:T(2,128)S(1)} %pad_maximum_fusion.17), channel_id=1, source_target_pairs={{240,0},{0,16},{16,32},{32,48},{48,64},{64,80},{80,96},{96,112},{1... | collective-permute-start | bytes 6152 | tf_op jit(solution)/shard_map/while/body/eval_jaxpr/ppermute | solution.py:18
  309.5 10.1 %collective-permute-start = (f32[2,256]{1,0:T(2,128)}, f32[2,256]{1,0:T(2,128)}, u32[]{:S(2)}, u32[]{:S(2)}) collective-permute-start(f32[2,256]{1,0:T(2,128)} %pad_maximum_fusion.14), channel_id=1, source_target_pairs={{16,0},{32,16},{48,32},{64,48},{80,64},{96,80},{112,96},{128,112},... | collective-permute-start | bytes 6152 | tf_op jit(solution)/shard_map/while/body/eval_jaxpr/ppermute | solution.py:18
  320.9 6.9 %collective-permute-start.3 = (f32[2,256]{1,0:T(2,128)S(1)}, f32[2,256]{1,0:T(2,128)S(1)}, u32[]{:S(2)}, u32[]{:S(2)}) collective-permute-start(f32[2,256]{1,0:T(2,128)S(1)} %pad_maximum_fusion.17), channel_id=1, source_target_pairs={{240,0},{0,16},{16,32},{32,48},{48,64},{64,80},{80,96},{96,112},{1... | collective-permute-start | bytes 6152 | tf_op jit(solution)/shard_map/while/body/eval_jaxpr/ppermute | solution.py:18
  334.5 10.1 %collective-permute-start = (f32[2,256]{1,0:T(2,128)}, f32[2,256]{1,0:T(2,128)}, u32[]{:S(2)}, u32[]{:S(2)}) collective-permute-start(f32[2,256]{1,0:T(2,128)} %pad_maximum_fusion.14), channel_id=1, source_target_pairs={{16,0},{32,16},{48,32},{64,48},{80,64},{96,80},{112,96},{128,112},... | collective-permute-start | bytes 6152 | tf_op jit(solution)/shard_map/while/body/eval_jaxpr/ppermute | solution.py:18
  345.9 6.9 %collective-permute-start.3 = (f32[2,256]{1,0:T(2,128)S(1)}, f32[2,256]{1,0:T(2,128)S(1)}, u32[]{:S(2)}, u32[]{:S(2)}) collective-permute-start(f32[2,256]{1,0:T(2,128)S(1)} %pad_maximum_fusion.17), channel_id=1, source_target_pairs={{240,0},{0,16},{16,32},{32,48},{48,64},{64,80},{80,96},{96,112},{1... | collective-permute-start | bytes 6152 | tf_op jit(solution)/shard_map/while/body/eval_jaxpr/ppermute | solution.py:18
  359.5 10.1 %collective-permute-start = (f32[2,256]{1,0:T(2,128)}, f32[2,256]{1,0:T(2,128)}, u32[]{:S(2)}, u32[]{:S(2)}) collective-permute-start(f32[2,256]{1,0:T(2,128)} %pad_maximum_fusion.14), channel_id=1, source_target_pairs={{16,0},{32,16},{48,32},{64,48},{80,64},{96,80},{112,96},{128,112},... | collective-permute-start | bytes 6152 | tf_op jit(solution)/shard_map/while/body/eval_jaxpr/ppermute | solution.py:18
  370.9 6.9 %collective-permute-start.3 = (f32[2,256]{1,0:T(2,128)S(1)}, f32[2,256]{1,0:T(2,128)S(1)}, u32[]{:S(2)}, u32[]{:S(2)}) collective-permute-start(f32[2,256]{1,0:T(2,128)S(1)} %pad_maximum_fusion.17), channel_id=1, source_target_pairs={{240,0},{0,16},{16,32},{32,48},{48,64},{64,80},{80,96},{96,112},{1... | collective-permute-start | bytes 6152 | tf_op jit(solution)/shard_map/while/body/eval_jaxpr/ppermute | solution.py:18
  384.5 10.1 %collective-permute-start = (f32[2,256]{1,0:T(2,128)}, f32[2,256]{1,0:T(2,128)}, u32[]{:S(2)}, u32[]{:S(2)}) collective-permute-start(f32[2,256]{1,0:T(2,128)} %pad_maximum_fusion.14), channel_id=1, source_target_pairs={{16,0},{32,16},{48,32},{64,48},{80,64},{96,80},{112,96},{128,112},... | collective-permute-start | bytes 6152 | tf_op jit(solution)/shard_map/while/body/eval_jaxpr/ppermute | solution.py:18
  395.9 6.9 %collective-permute-start.3 = (f32[2,256]{1,0:T(2,128)S(1)}, f32[2,256]{1,0:T(2,128)S(1)}, u32[]{:S(2)}, u32[]{:S(2)}) collective-permute-start(f32[2,256]{1,0:T(2,128)S(1)} %pad_maximum_fusion.17), channel_id=1, source_target_pairs={{240,0},{0,16},{16,32},{32,48},{48,64},{64,80},{80,96},{96,112},{1... | collective-permute-start | bytes 6152 | tf_op jit(solution)/shard_map/while/body/eval_jaxpr/ppermute | solution.py:18
  409.5 10.1 %collective-permute-start = (f32[2,256]{1,0:T(2,128)}, f32[2,256]{1,0:T(2,128)}, u32[]{:S(2)}, u32[]{:S(2)}) collective-permute-start(f32[2,256]{1,0:T(2,128)} %pad_maximum_fusion.14), channel_id=1, source_target_pairs={{16,0},{32,16},{48,32},{64,48},{80,64},{96,80},{112,96},{128,112},... | collective-permute-start | bytes 6152 | tf_op jit(solution)/shard_map/while/body/eval_jaxpr/ppermute | solution.py:18
  420.9 6.9 %collective-permute-start.3 = (f32[2,256]{1,0:T(2,128)S(1)}, f32[2,256]{1,0:T(2,128)S(1)}, u32[]{:S(2)}, u32[]{:S(2)}) collective-permute-start(f32[2,256]{1,0:T(2,128)S(1)} %pad_maximum_fusion.17), channel_id=1, source_target_pairs={{240,0},{0,16},{16,32},{32,48},{48,64},{64,80},{80,96},{96,112},{1... | collective-permute-start | bytes 6152 | tf_op jit(solution)/shard_map/while/body/eval_jaxpr/ppermute | solution.py:18
  434.5 10.1 %collective-permute-start = (f32[2,256]{1,0:T(2,128)}, f32[2,256]{1,0:T(2,128)}, u32[]{:S(2)}, u32[]{:S(2)}) collective-permute-start(f32[2,256]{1,0:T(2,128)} %pad_maximum_fusion.14), channel_id=1, source_target_pairs={{16,0},{32,16},{48,32},{64,48},{80,64},{96,80},{112,96},{128,112},... | collective-permute-start | bytes 6152 | tf_op jit(solution)/shard_map/while/body/eval_jaxpr/ppermute | solution.py:18
  445.9 6.9 %collective-permute-start.3 = (f32[2,256]{1,0:T(2,128)S(1)}, f32[2,256]{1,0:T(2,128)S(1)}, u32[]{:S(2)}, u32[]{:S(2)}) collective-permute-start(f32[2,256]{1,0:T(2,128)S(1)} %pad_maximum_fusion.17), channel_id=1, source_target_pairs={{240,0},{0,16},{16,32},{32,48},{48,64},{64,80},{80,96},{96,112},{1... | collective-permute-start | bytes 6152 | tf_op jit(solution)/shard_map/while/body/eval_jaxpr/ppermute | solution.py:18
  459.5 10.1 %collective-permute-start = (f32[2,256]{1,0:T(2,128)}, f32[2,256]{1,0:T(2,128)}, u32[]{:S(2)}, u32[]{:S(2)}) collective-permute-start(f32[2,256]{1,0:T(2,128)} %pad_maximum_fusion.14), channel_id=1, source_target_pairs={{16,0},{32,16},{48,32},{64,48},{80,64},{96,80},{112,96},{128,112},... | collective-permute-start | bytes 6152 | tf_op jit(solution)/shard_map/while/body/eval_jaxpr/ppermute | solution.py:18
  470.9 6.9 %collective-permute-start.3 = (f32[2,256]{1,0:T(2,128)S(1)}, f32[2,256]{1,0:T(2,128)S(1)}, u32[]{:S(2)}, u32[]{:S(2)}) collective-permute-start(f32[2,256]{1,0:T(2,128)S(1)} %pad_maximum_fusion.17), channel_id=1, source_target_pairs={{240,0},{0,16},{16,32},{32,48},{48,64},{64,80},{80,96},{96,112},{1... | collective-permute-start | bytes 6152 | tf_op jit(solution)/shard_map/while/body/eval_jaxpr/ppermute | solution.py:18
  484.5 10.1 %collective-permute-start = (f32[2,256]{1,0:T(2,128)}, f32[2,256]{1,0:T(2,128)}, u32[]{:S(2)}, u32[]{:S(2)}) collective-permute-start(f32[2,256]{1,0:T(2,128)} %pad_maximum_fusion.14), channel_id=1, source_target_pairs={{16,0},{32,16},{48,32},{64,48},{80,64},{96,80},{112,96},{128,112},... | collective-permute-start | bytes 6152 | tf_op jit(solution)/shard_map/while/body/eval_jaxpr/ppermute | solution.py:18
  495.9 6.9 %collective-permute-start.3 = (f32[2,256]{1,0:T(2,128)S(1)}, f32[2,256]{1,0:T(2,128)S(1)}, u32[]{:S(2)}, u32[]{:S(2)}) collective-permute-start(f32[2,256]{1,0:T(2,128)S(1)} %pad_maximum_fusion.17), channel_id=1, source_target_pairs={{240,0},{0,16},{16,32},{32,48},{48,64},{64,80},{80,96},{96,112},{1... | collective-permute-start | bytes 6152 | tf_op jit(solution)/shard_map/while/body/eval_jaxpr/ppermute | solution.py:18
  509.5 10.1 %collective-permute-start = (f32[2,256]{1,0:T(2,128)}, f32[2,256]{1,0:T(2,128)}, u32[]{:S(2)}, u32[]{:S(2)}) collective-permute-start(f32[2,256]{1,0:T(2,128)} %pad_maximum_fusion.14), channel_id=1, source_target_pairs={{16,0},{32,16},{48,32},{64,48},{80,64},{96,80},{112,96},{128,112},... | collective-permute-start | bytes 6152 | tf_op jit(solution)/shard_map/while/body/eval_jaxpr/ppermute | solution.py:18
  520.9 6.9 %collective-permute-start.3 = (f32[2,256]{1,0:T(2,128)S(1)}, f32[2,256]{1,0:T(2,128)S(1)}, u32[]{:S(2)}, u32[]{:S(2)}) collective-permute-start(f32[2,256]{1,0:T(2,128)S(1)} %pad_maximum_fusion.17), channel_id=1, source_target_pairs={{240,0},{0,16},{16,32},{32,48},{48,64},{64,80},{80,96},{96,112},{1... | collective-permute-start | bytes 6152 | tf_op jit(solution)/shard_map/while/body/eval_jaxpr/ppermute | solution.py:18
  534.5 10.1 %collective-permute-start = (f32[2,256]{1,0:T(2,128)}, f32[2,256]{1,0:T(2,128)}, u32[]{:S(2)}, u32[]{:S(2)}) collective-permute-start(f32[2,256]{1,0:T(2,128)} %pad_maximum_fusion.14), channel_id=1, source_target_pairs={{16,0},{32,16},{48,32},{64,48},{80,64},{96,80},{112,96},{128,112},... | collective-permute-start | bytes 6152 | tf_op jit(solution)/shard_map/while/body/eval_jaxpr/ppermute | solution.py:18
  545.9 6.9 %collective-permute-start.3 = (f32[2,256]{1,0:T(2,128)S(1)}, f32[2,256]{1,0:T(2,128)S(1)}, u32[]{:S(2)}, u32[]{:S(2)}) collective-permute-start(f32[2,256]{1,0:T(2,128)S(1)} %pad_maximum_fusion.17), channel_id=1, source_target_pairs={{240,0},{0,16},{16,32},{32,48},{48,64},{64,80},{80,96},{96,112},{1... | collective-permute-start | bytes 6152 | tf_op jit(solution)/shard_map/while/body/eval_jaxpr/ppermute | solution.py:18
  559.5 10.1 %collective-permute-start = (f32[2,256]{1,0:T(2,128)}, f32[2,256]{1,0:T(2,128)}, u32[]{:S(2)}, u32[]{:S(2)}) collective-permute-start(f32[2,256]{1,0:T(2,128)} %pad_maximum_fusion.14), channel_id=1, source_target_pairs={{16,0},{32,16},{48,32},{64,48},{80,64},{96,80},{112,96},{128,112},... | collective-permute-start | bytes 6152 | tf_op jit(solution)/shard_map/while/body/eval_jaxpr/ppermute | solution.py:18
  584.5 10.1 %collective-permute-start = (f32[2,256]{1,0:T(2,128)}, f32[2,256]{1,0:T(2,128)}, u32[]{:S(2)}, u32[]{:S(2)}) collective-permute-start(f32[2,256]{1,0:T(2,128)} %pad_maximum_fusion.14), channel_id=1, source_target_pairs={{16,0},{32,16},{48,32},{64,48},{80,64},{96,80},{112,96},{128,112},... | collective-permute-start | bytes 6152 | tf_op jit(solution)/shard_map/while/body/eval_jaxpr/ppermute | solution.py:18
  619.3 8.1 %collective-permute-start.6 = (f32[262,3]{1,0:T(8,128)S(1)}, f32[262,3]{1,0:T(8,128)S(1)}, u32[]{:S(2)}, u32[]{:S(2)}) collective-permute-start(f32[262,3]{1,0:T(8,128)S(1)} %get-tuple-element.211), channel_id=1, source_target_pairs={{0,1},{1,2},{2,3},{3,4},{4,5},{5,6},{6,7},{7,8},{8,9},{9,10},{10,1... | collective-permute-start | bytes 9440 | tf_op jit(solution)/shard_map/ppermute | solution.py:28
  619.4 8.0 %collective-permute-start.7 = (f32[262,3]{1,0:T(8,128)S(1)}, f32[262,3]{1,0:T(8,128)S(1)}, u32[]{:S(2)}, u32[]{:S(2)}) collective-permute-start(f32[262,3]{1,0:T(8,128)S(1)} %get-tuple-element.212), channel_id=1, source_target_pairs={{1,0},{2,1},{3,2},{4,3},{5,4},{6,5},{7,6},{8,7},{9,8},{10,9},{11,1... | collective-permute-start | bytes 9440 | tf_op jit(solution)/shard_map/ppermute | solution.py:29
  (296 other events, 1135.5 us)
where the time goes:
time: 636 us; the launch traced here: 630 us
  local copies, waits for them, and re-layouts  247 us (39%)
  other arithmetic  139 us (22%)
  starting transfers between devices  126 us (20%)
  waiting for transfers between devices  111 us (17%)
  loops' own time  6.66 us (1%)
    ppermute x96, starting transfers between devices, shifted(): return lax.ppermute(block, axis, route)  116 us
    ppermute x96, waiting for transfers between devices, shifted(): return lax.ppermute(block, axis, route)  107 us
    while x552, local copies, waits for them, and re-layouts  90.8 us
    concatenate x216, local copies, waits for them, and re-layouts, with_edge(): rolled = jnp.roll(plane, -step, dim)  48.9 us
    div x24, local copies, waits for them, and re-layouts, accumulate(): coefs = jnp.stack([jnp.cos(theta), jnp.sin(theta)], axis=1) / STEPS  30.6 us
    sub x24, other arithmetic, update_h(): hx = hx - courant * (ez_ny - ez)  24.9 us
    add x24, other arithmetic, accumulate(): return acc + coefs[:, :, None, None, None] * efield[None, None]  23.8 us
    slice x24, local copies, waits for them, and re-layouts, with_edge(): rolled = jnp.roll(plane, -step, dim)  19 us
  transfers between devices with their start and end apart: 100, of which 27 were waited for; matrix products, arithmetic and copies ran while one was open for 30% of the time, Pallas kernels for 0%

commit v1 on v0

v1 whole, which is shorter than its diff:
```python
import functools

import jax
import jax.numpy as jnp
import numpy as np
from jax import lax
from jax.experimental import pallas as pl
from jax.experimental.pallas import tpu as pltpu
from jax.sharding import PartitionSpec as P

STEPS = 24
NF = 3
RADIUS = 3
COURANT = 0.68

T = 256
PAD = 32
ROWS = T + 2 * PAD
CHUNK = 39
FIRST = (ROWS - 8 * CHUNK) // 2
LANES = 128
DEEP = STEPS + 2
PLANES = 6 * NF
K = 8 * 2 * NF

f32 = jnp.float32
bf16 = jnp.bfloat16


def filter_table():
    offsets = np.arange(-RADIUS, RADIUS + 1)
    dist = np.sqrt(offsets[:, None] ** 2 + offsets[None, :] ** 2)
    table = np.maximum(0.0, RADIUS - dist)
    return table / table.sum()


def lane_iota():
    return lax.broadcasted_iota(jnp.int32, (8, LANES), 1)


def turn(x, shift, axis):
    size = x.shape[axis]
    shift = shift % size
    return x if shift == 0 else pltpu.roll(x, shift, axis)


def left_slot(group):
    return 32 * ((group + 1) % 4)


def pack_kernel(fields, inv_eps, fwd, mask, xs0, xs1, ys0, ys1, f7, fw, mk, xbuf, ybuf, sems):
    px = lax.rem(lax.axis_index("gx"), 2)
    py = lax.rem(lax.axis_index("gy"), 2)
    loads = [
        pltpu.make_async_copy(fields, f7.at[pl.ds(0, 6)], sems.at[0]),
        pltpu.make_async_copy(inv_eps, f7.at[6], sems.at[1]),
        pltpu.make_async_copy(mask, mk, sems.at[2]),
        pltpu.make_async_copy(fwd, fw.at[pl.ds(0, PLANES)], sems.at[3]),
    ]
    for copy in loads:
        copy.start()
    for copy in loads:
        copy.wait()
    fw[PLANES] = mk[...].astype(f32)

    sub = lax.broadcasted_iota(jnp.int32, (8, T), 0)
    for k in range(7):
        extra = [m for m in range(3 * k, 3 * k + 3) if m <= PLANES]
        xbuf[0, k, pl.ds(8, 24)] = f7[k, pl.ds(T - 24, 24)]
        xbuf[1, k, pl.ds(0, 24)] = f7[k, pl.ds(0, 24)]
        low, high = f7[k, pl.ds(T - 32, 8)], f7[k, pl.ds(24, 8)]
        for jj, m in enumerate(extra):
            low = jnp.where(sub // 2 == jj, turn(fw[m, pl.ds(T - 8, 8)], 2 * jj + 2, 0), low)
            high = jnp.where(sub // 2 == jj + 1, turn(fw[m, pl.ds(0, 8)], 2 * jj + 2, 0), high)
        xbuf[0, k, pl.ds(0, 8)] = low
        xbuf[1, k, pl.ds(24, 8)] = high

    lane = lane_iota()

    def rows(j, _):
        for k in range(7):
            extra = [m for m in range(3 * k, 3 * k + 3) if m <= PLANES]
            last = first = jnp.zeros((8, LANES), f32)
            for g in range(4):
                at = pl.ds(pl.multiple_of(64 * g + 8 * j, 8), 8)
                a = f7[k, at, pl.ds(0, LANES)]
                b = f7[k, at, pl.ds(LANES, LANES)]
                for jj, m in enumerate(extra):
                    fa = fw[m, at, pl.ds(0, LANES)]
                    fb = fw[m, at, pl.ds(LANES, LANES)]
                    a = jnp.where(lane // 2 == 13 + jj, turn(fa, 26 + 2 * jj, 1), a)
                    b = jnp.where(lane // 2 == 48 + jj, turn(fb, 98 + 2 * jj, 1), b)
                first = jnp.where(lane // 32 == g, turn(a, 32 * g, 1), first)
                last = jnp.where(lane // 32 == (g + 1) % 4, turn(b, left_slot(g) - 96, 1), last)
            to = pl.ds(pl.multiple_of(8 * j, 8), 8)
            ybuf[0, k, to] = last
            ybuf[1, k, to] = first
        return 0

    lax.fori_loop(0, 8, rows, 0)
    stores = [
        pltpu.make_async_copy(xbuf.at[px], xs0, sems.at[0]),
        pltpu.make_async_copy(xbuf.at[1 - px], xs1, sems.at[1]),
        pltpu.make_async_copy(ybuf.at[py], ys0, sems.at[2]),
        pltpu.make_async_copy(ybuf.at[1 - py], ys1, sems.at[3]),
    ]
    for copy in stores:
        copy.start()
    for copy in stores:
        copy.wait()


def pack(fields, inv_eps, fwd, mask):
    any_space = pl.BlockSpec(memory_space=pl.ANY)
    x_slab = jax.ShapeDtypeStruct((7, 32, T), f32)
    y_slab = jax.ShapeDtypeStruct((7, 64, LANES), f32)
    return pl.pallas_call(
        pack_kernel,
        out_shape=(x_slab, x_slab, y_slab, y_slab),
        in_specs=[any_space] * 4,
        out_specs=(any_space,) * 4,
        scratch_shapes=[
            pltpu.VMEM((7, T, T), f32),
            pltpu.VMEM((PLANES + 1, T, T), f32),
            pltpu.VMEM((T, T), jnp.int32),
            pltpu.VMEM((2, 7, 32, T), f32),
            pltpu.VMEM((2, 7, 64, LANES), f32),
            pltpu.SemaphoreType.DMA((4,)),
        ],
        compiler_params=pltpu.CompilerParams(vmem_limit_bytes=24 * 2**20),
        name="pack",
    )(fields, inv_eps, fwd, mask)


def next_lane(tiles, lane):
    r = [turn(x, -1, 1) for x in tiles]
    return [jnp.where(lane == LANES - 1, r[(t + 1) % 3], r[t]) for t in range(3)]


def prev_lane(tiles, lane):
    r = [turn(x, 1, 1) for x in tiles]
    return [jnp.where(lane == 0, r[(t + 2) % 3], r[t]) for t in range(3)]


def main_kernel(coef, fields, inv_eps, fwd, mask, x0, x1, y0, y1, c0, c1, out, grad,
                stage, fst, mk, yl, yr, cl, ch, e, h, fac, raw, sems):
    px = lax.rem(lax.axis_index("gx"), 2)
    py = lax.rem(lax.axis_index("gy"), 2)
    own = pl.ds(PAD, T)
    copies, late = [], []
    for t in range(2):
        cols = pl.ds(LANES * t, LANES)
        copies.append(pltpu.make_async_copy(fields.at[:, :, cols], stage.at[pl.ds(0, 6), t, own], sems.at[t]))
        copies.append(pltpu.make_async_copy(inv_eps.at[:, cols], stage.at[6, t, own], sems.at[2 + t]))
        late.append(pltpu.make_async_copy(fwd.at[:, :, cols], fst.at[pl.ds(0, PLANES), t, own], sems.at[4 + t]))
    late.append(pltpu.make_async_copy(mask, mk, sems.at[6]))

    def edges(low, high, left, right, clow, chigh):
        res = []
        for t in range(2):
            cols = pl.ds(LANES * t, LANES)
            res.append(pltpu.make_async_copy(low.at[:, :, cols], stage.at[:, t, pl.ds(0, PAD)], sems.at[7 + t]))
            res.append(pltpu.make_async_copy(high.at[:, :, cols], stage.at[:, t, pl.ds(PAD + T, PAD)], sems.at[9 + t]))
        res.append(pltpu.make_async_copy(left, yl, sems.at[11]))
        res.append(pltpu.make_async_copy(right, yr, sems.at[12]))
        res.append(pltpu.make_async_copy(clow, cl, sems.at[13]))
        res.append(pltpu.make_async_copy(chigh, ch, sems.at[14]))
        return res

    for copy in copies:
        copy.start()
    for ix in range(2):
        for iy in range(2):
            @pl.when((px == ix) & (py == iy))
            def _():
                xs = (x1, x0) if ix == 0 else (x0, x1)
                ys = (y1, y0) if iy == 0 else (y0, y1)
                cs = (c1, c0) if ix == 0 else (c0, c1)
                for copy in edges(*xs, *ys, *cs):
                    copy.start()
    for copy in late:
        copy.start()
    for copy in copies:
        copy.wait()
    for copy in edges(x0, x1, y0, y1, c0, c1):
        copy.wait()

    lane = lane_iota()
    sub = lax.broadcasted_iota(jnp.int32, (8, LANES), 0)
    right_half = lane < 64

    def fill(j, _):
        at = pl.ds(pl.multiple_of(8 * j, 8), 8)
        for k in range(7):
            r, l = yr[k, at], yl[k, at]
            for g in range(4):
                to = pl.ds(pl.multiple_of(PAD + 64 * g + 8 * j, 8), 8)
                stage[k, 2, to] = jnp.where(right_half, turn(r, -32 * g, 1), turn(l, 96 - left_slot(g), 1))
                for jj, m in enumerate(range(3 * k, min(3 * k + 3, PLANES + 1))):
                    fst[m, 2, to] = jnp.where(
                        right_half, turn(r, -32 * g - 26 - 2 * jj, 1), turn(l, 126 - left_slot(g) - 2 * jj, 1)
                    )
        return 0

    lax.fori_loop(0, 8, fill, 0)
    zero = jnp.zeros((8, LANES), f32)
    for k in range(7):
        for j in range(4):
            a, b = cl[k, pl.ds(8 * j, 8)], ch[k, pl.ds(8 * j, 8)]
            stage[k, 2, pl.ds(8 * j, 8)] = jnp.where(right_half, turn(a, 32, 1), turn(a, 96, 1))
            stage[k, 2, pl.ds(PAD + T + 8 * j, 8)] = jnp.where(right_half, b, turn(b, 64, 1))
        a, b = cl[k, pl.ds(24, 8)], ch[k, pl.ds(0, 8)]
        for jj, m in enumerate(range(3 * k, min(3 * k + 3, PLANES + 1))):
            fst[m, 2, pl.ds(24, 8)] = jnp.where(right_half, turn(a, 32 - 26 - 2 * jj, 1), turn(a, 126 - 2 * jj, 1))
            fst[m, 2, pl.ds(PAD + T, 8)] = jnp.where(right_half, turn(b, -26 - 2 * jj, 1), turn(b, 94 - 2 * jj, 1))
            for t in range(2):
                lo, hi = stage[k, t, pl.ds(0, 8)], stage[k, t, pl.ds(ROWS - 8, 8)]
                fst[m, t, pl.ds(24, 8)] = jnp.where(sub >= 6, turn(lo, 6 - 2 * jj, 0), 0.0)
                fst[m, t, pl.ds(PAD + T, 8)] = jnp.where(sub < 2, turn(hi, -2 - 2 * jj, 0), 0.0)
            for t in range(3):
                for j in range(3):
                    fst[m, t, pl.ds(8 * j, 8)] = zero
                    fst[m, t, pl.ds(PAD + T + 8 + 8 * j, 8)] = zero

    def lift(v, _):
        at = pl.ds(FIRST + v, 8, stride=CHUNK)
        for t in range(3):
            for c in range(3):
                e[0, c, v, t] = stage[c, t, at, :]
                h[c, v, t] = stage[3 + c, t, at, :] * (1.0 / COURANT)
            fac[v, t] = stage[6, t, at, :] * (COURANT * COURANT)
        return 0

    lax.fori_loop(0, CHUNK, lift, 0)

    def step(n, _):
        def load_e(c, v):
            return [e[n, c, v, t] for t in range(3)]

        def load_h(c, v):
            return [h[c, v, t] for t in range(3)]

        def electric(v, ex, ey, ez, hx, hy, hz, hy_p, hz_p):
            hz_py, hx_py = prev_lane(hz, lane), prev_lane(hx, lane)
            for t in range(3):
                f = fac[v, t]
                e[n + 1, 0, v, t] = ex[t] + f * (hz[t] - hz_py[t])
                e[n + 1, 1, v, t] = ey[t] - f * (hz[t] - hz_p[t])
                e[n + 1, 2, v, t] = ez[t] + f * ((hy[t] - hy_p[t]) - (hx[t] - hx_py[t]))

        ey, ez = load_e(1, 0), load_e(2, 0)
        end = ([turn(x, -1, 0) for x in ey], [turn(x, -1, 0) for x in ez])
        hy_p = hz_p = None
        for v in range(CHUNK):
            ex = load_e(0, v)
            ey_n, ez_n = (load_e(1, v + 1), load_e(2, v + 1)) if v < CHUNK - 1 else end
            ex_ny, ez_ny = next_lane(ex, lane), next_lane(ez, lane)
            hx, hy, hz = load_h(0, v), load_h(1, v), load_h(2, v)
            for t in range(3):
                hx[t] = hx[t] - (ez_ny[t] - ez[t])
                hy[t] = hy[t] + (ez_n[t] - ez[t])
                hz[t] = hz[t] - ((ey_n[t] - ey[t]) - (ex_ny[t] - ex[t]))
                h[0, v, t], h[1, v, t], h[2, v, t] = hx[t], hy[t], hz[t]
            if v > 0:
                electric(v, ex, ey, ez, hx, hy, hz, hy_p, hz_p)
            ey, ez, hy_p, hz_p = ey_n, ez_n, hy, hz
        hy_p, hz_p = [turn(x, 1, 0) for x in hy_p], [turn(x, 1, 0) for x in hz_p]
        electric(0, load_e(0, 0), load_e(1, 0), load_e(2, 0), load_h(0, 0), load_h(1, 0), load_h(2, 0), hy_p, hz_p)
        return 0

    lax.fori_loop(0, STEPS, step, 0)

    for copy in late:
        copy.wait()
    for t in range(2):
        fst[PLANES, t, own] = mk[:, pl.ds(LANES * t, LANES)].astype(f32)

    def lower(v, _):
        at = pl.ds(FIRST + v, 8, stride=CHUNK)
        for t in range(2):
            for c in range(3):
                stage[c, t, at, :] = e[STEPS, c, v, t]
                stage[3 + c, t, at, :] = h[c, v, t] * COURANT
        return 0

    lax.fori_loop(0, CHUNK, lower, 0)
    stores = [
        pltpu.make_async_copy(stage.at[pl.ds(0, 6), t, own], out.at[:, :, pl.ds(LANES * t, LANES)], sems.at[t])
        for t in range(2)
    ]
    for copy in stores:
        copy.start()

    def gather(v, _):
        at = pl.ds(FIRST + v, 8, stride=CHUNK)
        total = [zero] * 3
        for c in range(3):
            w = jnp.concatenate(
                [jnp.concatenate([fst[3 * i + c, t, at, :] for t in range(3)], axis=1) for i in range(2 * NF)], axis=0
            )
            hi = w.astype(bf16)
            lo = (w - hi.astype(f32)).astype(bf16)
            g = jnp.dot(coef[...], jnp.concatenate([hi, hi, lo], axis=0), preferred_element_type=f32)
            for n in range(STEPS):
                for t in range(3):
                    total[t] = total[t] + e[n + 1, c, v, t] * g[8 * n : 8 * n + 8, LANES * t : LANES * t + LANES]
        for t in range(3):
            raw[v + 2, t] = total[t] * fst[PLANES, t, at, :]
        return 0

    lax.fori_loop(0, CHUNK, gather, 0)
    for t in range(3):
        for v in range(2):
            raw[v, t] = turn(raw[CHUNK + v, t], 1, 0)
            raw[CHUNK + 2 + v, t] = turn(raw[2 + v, t], -1, 0)

    table = filter_table()

    def smooth(v, _):
        part = []
        for t in range(3):
            r0 = raw[v + 2, t]
            r1 = raw[v + 1, t] + raw[v + 3, t]
            r2 = raw[v, t] + raw[v + 4, t]
            part.append([
                float(table[3, 3 + b]) * r0 + float(table[4, 3 + b]) * r1 + float(table[5, 3 + b]) * r2 for b in range(3)
            ])
        at = pl.ds(FIRST + v, 8, stride=CHUNK)
        for t in range(2):
            acc = part[t][0]
            for b in (1, 2):
                up = jnp.where(lane >= LANES - b, turn(part[(t + 1) % 3][b], -b, 1), turn(part[t][b], -b, 1))
                down = jnp.where(lane < b, turn(part[(t + 2) % 3][b], b, 1), turn(part[t][b], b, 1))
                acc = acc + (up + down)
            stage[6, t, at, :] = acc
        return 0

    lax.fori_loop(0, CHUNK, smooth, 0)
    stores += [
        pltpu.make_async_copy(stage.at[6, t, own], grad.at[:, pl.ds(LANES * t, LANES)], sems.at[2 + t]) for t in range(2)
    ]
    for copy in stores[2:]:
        copy.start()
    for copy in stores:
        copy.wait()


def advance(coef, fields, inv_eps, fwd, mask, *edges):
    any_space = pl.BlockSpec(memory_space=pl.ANY)
    return pl.pallas_call(
        main_kernel,
        out_shape=(jax.ShapeDtypeStruct((6, T, T), f32), jax.ShapeDtypeStruct((T, T), f32)),
        in_specs=[pl.BlockSpec(memory_space=pltpu.VMEM)] + [any_space] * 10,
        out_specs=(any_space,) * 2,
        scratch_shapes=[
            pltpu.VMEM((7, 3, ROWS, LANES), f32),
            pltpu.VMEM((PLANES + 1, 3, ROWS, LANES), f32),
            pltpu.VMEM((T, T), jnp.int32),
            pltpu.VMEM((7, 64, LANES), f32),
            pltpu.VMEM((7, 64, LANES), f32),
            pltpu.VMEM((7, 32, LANES), f32),
            pltpu.VMEM((7, 32, LANES), f32),
            pltpu.VMEM((STEPS + 1, 3, CHUNK, 3, 8, LANES), f32),
            pltpu.VMEM((3, CHUNK, 3, 8, LANES), f32),
            pltpu.VMEM((CHUNK, 3, 8, LANES), f32),
            pltpu.VMEM((CHUNK + 4, 3, 8, LANES), f32),
            pltpu.SemaphoreType.DMA((15,)),
        ],
        compiler_params=pltpu.CompilerParams(vmem_limit_bytes=58 * 2**20),
        name="advance",
    )(coef, fields, inv_eps, fwd, mask, *edges)


def swap(x, axis, offset):
    count = lax.axis_size(axis)
    route = []
    for i in range(offset, count + offset, 2):
        a, b = i % count, (i + 1) % count
        route += [(a, b), (b, a)]
    return lax.ppermute(x, axis, route)


def coefficients(phase_start, omega):
    theta = phase_start[None] + omega[None] * jnp.arange(STEPS, dtype=f32)[:, None]
    table = jnp.stack([jnp.cos(theta), -jnp.sin(theta)], axis=2).reshape(STEPS, 2 * NF) / STEPS
    high = lax.reduce_precision(table, 8, 7)
    low = lax.reduce_precision(table - high, 8, 7)
    cols = jnp.concatenate([high, low, high], axis=1)
    wide = cols[:, None, :, None] * jnp.eye(8, dtype=f32)[None, :, None, :]
    return wide.reshape(STEPS * 8, 3 * K).astype(bf16)


def local(fields, inv_eps, fwd_dft, phase_start, omega, mask):
    fwd = fwd_dft.reshape(PLANES, T, T)
    coef = coefficients(phase_start, omega)
    xs0, xs1, ys0, ys1 = pack(fields, inv_eps, fwd, mask)
    y0 = swap(ys0, "gy", 0)
    x0 = swap(xs0, "gx", 0)
    y1 = swap(ys1, "gy", 1)
    x1 = swap(xs1, "gx", 1)
    even_x = lax.rem(lax.axis_index("gx"), 2) == 0
    even_y = lax.rem(lax.axis_index("gy"), 2) == 0
    right = jnp.where(even_y, y0, y1)
    left = jnp.where(even_y, y1, y0)
    lane = lax.broadcasted_iota(jnp.int32, (7, 32, LANES), 2)
    up = jnp.where(lane >= 96, right[:, 32:], left[:, 32:])
    down = jnp.where(lane < 32, right[:, :32], left[:, :32])
    c0 = swap(jnp.where(even_x, up, down), "gx", 0)
    c1 = swap(jnp.where(even_x, down, up), "gx", 1)
    return advance(coef, fields, inv_eps, fwd, mask, x0, x1, y0, y1, c0, c1)


def solution(mesh):
    return jax.shard_map(
        local,
        mesh=mesh,
        in_specs=(
            P(None, "gx", "gy"),
            P("gx", "gy"),
            P(None, None, None, "gx", "gy"),
            P(),
            P(),
            P("gx", "gy"),
        ),
        out_specs=(P(None, "gx", "gy"), P("gx", "gy")),
        check_vma=False,
    )
```

time: 636 us -> 120 us (0.19)
  local copies, waits for them, and re-layouts: 247 us -> 7.93 us
  other arithmetic: 139 us -> 0.45 us
  starting transfers between devices: 126 us -> 11.4 us
  waiting for transfers between devices: 111 us -> 11.2 us
  Pallas kernels: 0 us -> 87.8 us
  loops' own time: 6.66 us -> 0 us
    ppermute x100 -> x6, starting transfers between devices: 126 us -> 11.4 us  [swap(): return lax.ppermute(x, axis, route)]
    ppermute x100 -> x6, waiting for transfers between devices: 111 us -> 11.2 us  [swap(): return lax.ppermute(x, axis, route)]
    while x552 -> x0, local copies, waits for them, and re-layouts: 90.8 us -> none
    pallas_call x0 -> x2, Pallas kernels: none -> 87.8 us  [the longest x1 80.1 us: advance(): pl.pallas_call(main_kernel, out_shape=(jax.ShapeDtypeStruct((6, T, T), f3...]
    slice x194 -> x0, local copies, waits for them, and re-layouts: 74.1 us -> none  [the longest x24 19 us: with_edge(): rolled = jnp.roll(plane, -step, dim)]
    concatenate x216 -> x0, local copies, waits for them, and re-layouts: 48.9 us -> none  [with_edge(): rolled = jnp.roll(plane, -step, dim)]
    div x24 -> x1, local copies, waits for them, and re-layouts: 30.6 us -> 0.01 us  [coefficients(): jnp.stack([jnp.cos(theta), -jnp.sin(theta)], axis=2).reshape(STEPS, 2 * NF)]
    add x49 -> x0, other arithmetic: 30.5 us -> none  [the longest x24 23.8 us: accumulate(): return acc + coefs[:, :, None, None, None] * efield[None, None]]
  transfers between devices with their start and end apart: 100 -> 6, of which waited for: 27 -> 3; matrix products, arithmetic and copies ran while one was open for 30% -> 1% of each run, Pallas kernels for 0% -> 0%
where the time goes in v1:
time: 120 us
  Pallas kernels  87.8 us (73%)
  starting transfers between devices  11.4 us (10%)
  waiting for transfers between devices  11.2 us (9%)
  local copies, waits for them, and re-layouts  7.93 us (7%)
    pallas_call x1, Pallas kernels, advance(): pl.pallas_call(main_kernel, out_shape=(jax.ShapeDtypeStruct((6, T, T), f3...  80.1 us
    ppermute x6, starting transfers between devices, swap(): return lax.ppermute(x, axis, route)  11.4 us
    ppermute x6, waiting for transfers between devices, swap(): return lax.ppermute(x, axis, route)  11.2 us
    pallas_call x1, Pallas kernels, pack(): pl.pallas_call(pack_kernel, out_shape=(x_slab, x_slab, y_slab, y_slab), i...  7.74 us
    unnamed x24, local copies, waits for them, and re-layouts  6.63 us
  transfers between devices with their start and end apart: 6, of which 3 were waited for; matrix products, arithmetic and copies ran while one was open for 1% of the time, Pallas kernels for 0%

profile of v1, /device:TPU:16, one launch (start us, length us, event | category | flops | bytes accessed | tf_op | source)
XLA Modules:
  0.0 119.7 jit_solution(3774144081927230305)
XLA Ops:
  0.6 0.0 copy-start
  0.6 2.3 %copy-done = f32[3,2,3,256,256]{4,3,2,1,0:T(8,128)S(1)} copy-done((f32[3,2,3,256,256]{4,3,2,1,0:T(8,128)S(1)}, f32[3,2,3,256,256]{4,3,2,1,0:T(8,128)}, u32[]{:S(2)}) %copy-start) | copy-done | bytes 4718616
  3.0 0.0 copy-start.1
  3.0 1.4 %copy-done.1 = f32[6,256,256]{2,1,0:T(8,128)S(1)} copy-done((f32[6,256,256]{2,1,0:T(8,128)S(1)}, f32[6,256,256]{2,1,0:T(8,128)}, u32[]{:S(2)}) %copy-start.1) | copy-done | bytes 1572888
  4.4 0.0 copy-start.2
  4.4 0.9 copy-done.2
  5.3 0.0 copy-start.3
  5.3 0.9 copy-done.3
  6.3 0.0 copy-start.10
  6.3 0.0 copy-start.11
  6.3 7.7 %pack.1 = (f32[7,32,256]{2,1,0:T(8,128)S(1)}, f32[7,32,256]{2,1,0:T(8,128)S(1)}, f32[7,64,128]{2,1,0:T(8,128)S(1)}, f32[7,64,128]{2,1,0:T(8,128)S(1)}) custom-call(f32[6,256,256]{2,1,0:T(8,128)S(1)} %copy-done.1, f32[256,256]{1,0:T(8,128)S(1)} %copy-done.2, f32[18,256,256]{2,1,0:T(8,128)S(1)} %bitcast.8, s32[256,256]{1,0:T(8,128)S(1)} %copy-done.3), custom_call_target="tpu_custom_call" | custom-call | tf_op jit(solution)/shard_map/pack/pallas_call | solution.py:117
  14.0 1.4 %collective-permute-start = (f32[7,32,256]{2,1,0:T(8,128)S(1)}, f32[7,32,256]{2,1,0:T(8,128)S(1)}, u32[]{:S(2)}, u32[]{:S(2)}) collective-permute-start(f32[7,32,256]{2,1,0:T(8,128)S(1)} %get-tuple-element.6), channel_id=1, source_target_pairs={{0,16},{16,0},{32,48},{48,32},{64,80},{80,64},{96,112},{112,96},{1... | collective-permute-start | bytes 688136 | tf_op jit(solution)/shard_map/ppermute | solution.py:380
  15.4 6.0 %collective-permute-start.1 = (f32[7,32,256]{2,1,0:T(8,128)S(1)}, f32[7,32,256]{2,1,0:T(8,128)S(1)}, u32[]{:S(2)}, u32[]{:S(2)}) collective-permute-start(f32[7,32,256]{2,1,0:T(8,128)S(1)} %get-tuple-element.7), channel_id=1, source_target_pairs={{16,32},{32,16},{48,64},{64,48},{80,96},{96,80},{112,128},{128,112... | collective-permute-start | bytes 688136 | tf_op jit(solution)/shard_map/ppermute | solution.py:380
  21.4 0.0 collective-permute-start.2
  21.4 2.6 %collective-permute-start.3 = (f32[7,64,128]{2,1,0:T(8,128)S(1)}, f32[7,64,128]{2,1,0:T(8,128)S(1)}, u32[]{:S(2)}, u32[]{:S(2)}) collective-permute-start(f32[7,64,128]{2,1,0:T(8,128)S(1)} %get-tuple-element.9), channel_id=1, source_target_pairs={{1,2},{2,1},{3,4},{4,3},{5,6},{6,5},{7,8},{8,7},{9,10},{10,9},{11,... | collective-permute-start | bytes 688136 | tf_op jit(solution)/shard_map/ppermute | solution.py:380
  24.1 0.0 copy-done.10
  24.1 0.0 copy-done.11
  24.1 0.1 fusion.1
  24.3 0.0 collective-permute-done.2.y0
  24.3 0.0 copy-start.4
  24.3 6.8 %collective-permute-done.3.y1 = f32[7,64,128]{2,1,0:T(8,128)S(1)} collective-permute-done((f32[7,64,128]{2,1,0:T(8,128)S(1)}, f32[7,64,128]{2,1,0:T(8,128)S(1)}, u32[]{:S(2)}, u32[]{:S(2)}) %collective-permute-start.3) | collective-permute-done | bytes 229408 | tf_op jit(solution)/shard_map/ppermute | solution.py:380
  31.1 0.0 copy-start.5
  31.2 1.4 %collective-permute-start.5 = (f32[7,32,128]{2,1,0:T(8,128)S(1)}, f32[7,32,128]{2,1,0:T(8,128)S(1)}, u32[]{:S(2)}, u32[]{:S(2)}) collective-permute-start(f32[7,32,128]{2,1,0:T(8,128)S(1)} %get-tuple-element.10), channel_id=1, source_target_pairs={{16,32},{32,16},{48,64},{64,48},{80,96},{96,80},{112,128},{128,112... | collective-permute-start | bytes 344072 | tf_op jit(solution)/shard_map/ppermute | solution.py:380
  32.6 0.0 collective-permute-start.4
  32.6 0.2 multiply_convert_fusion
  32.8 0.5 convert_element_type.14
  33.4 0.7 copy.8.coef
  34.1 0.0 copy-done.4
  34.1 0.0 copy-done.5
  34.1 0.0 collective-permute-done.x0
  34.1 0.0 copy-start.6
  34.1 0.0 collective-permute-done.1.x1
  34.1 0.0 copy-start.7
  34.1 4.1 %collective-permute-done.5.c1 = f32[7,32,128]{2,1,0:T(8,128)S(1)} collective-permute-done((f32[7,32,128]{2,1,0:T(8,128)S(1)}, f32[7,32,128]{2,1,0:T(8,128)S(1)}, u32[]{:S(2)}, u32[]{:S(2)}) %collective-permute-start.5) | collective-permute-done | bytes 114720 | tf_op jit(solution)/shard_map/ppermute | solution.py:380
  38.3 0.0 copy-start.8
  38.3 0.3 collective-permute-done.4.c0
  38.6 0.0 copy-done.6
  38.6 0.0 copy-done.7
  38.6 0.3 copy-done.8
  38.9 0.0 copy-start.9
  38.9 0.6 copy-done.9
  39.6 80.1 %advance.1 = (f32[6,256,256]{2,1,0:T(8,128)}, f32[256,256]{1,0:T(8,128)}) custom-call(bf16[192,144]{1,0:T(8,128)(2,1)} %copy.8.coef, f32[6,256,256]{2,1,0:T(8,128)} %fields.3, f32[256,256]{1,0:T(8,128)} %inv_eps.3, f32[18,256,256]{2,1,0:T(8,128)} %bitcast.7, s32[256,256]{1,0:T(8,128)} %mask.3, f32[7,32,256]{2,1,0:T(8,128)} %copy-done.6, ...), custom_call_target="tpu_custom_call" | custom-call | tf_op jit(solution)/shard_map/advance/pallas_call | solution.py:350
  (8 shorter events, 0.1 us)
Async XLA Ops:
  0.6 2.3 %copy-start = (f32[3,2,3,256,256]{4,3,2,1,0:T(8,128)S(1)}, f32[3,2,3,256,256]{4,3,2,1,0:T(8,128)}, u32[]{:S(2)}) copy-start(f32[3,2,3,256,256]{4,3,2,1,0:T(8,128)} %param.8) | copy-start | bytes 14155780
  3.0 1.4 %copy-start.1 = (f32[6,256,256]{2,1,0:T(8,128)S(1)}, f32[6,256,256]{2,1,0:T(8,128)}, u32[]{:S(2)}) copy-start(f32[6,256,256]{2,1,0:T(8,128)} %fields.3) | copy-start | bytes 4718596
  4.4 0.9 copy-start.2
  5.3 0.9 copy-start.3
  6.3 17.8 %copy-start.10 = (f32[3]{0:T(128)S(1)}, f32[3]{0:T(128)}, u32[]{:S(2)}) copy-start(f32[3]{0:T(128)} %param.10) | copy-start | bytes 40
  6.3 17.8 %copy-start.11 = (f32[3]{0:T(128)S(1)}, f32[3]{0:T(128)}, u32[]{:S(2)}) copy-start(f32[3]{0:T(128)} %param.9) | copy-start | bytes 40
  14.0 20.1 %collective-permute-start = (f32[7,32,256]{2,1,0:T(8,128)S(1)}, f32[7,32,256]{2,1,0:T(8,128)S(1)}, u32[]{:S(2)}, u32[]{:S(2)}) collective-permute-start(f32[7,32,256]{2,1,0:T(8,128)S(1)} %get-tuple-element.6), channel_id=1, source_target_pairs={{0,16},{16,0},{32,48},{48,32},{64,80},{80,64},{96,112},{112,96},{1... | collective-permute-start | bytes 688136 | tf_op jit(solution)/shard_map/ppermute | solution.py:380
  15.4 18.7 %collective-permute-start.1 = (f32[7,32,256]{2,1,0:T(8,128)S(1)}, f32[7,32,256]{2,1,0:T(8,128)S(1)}, u32[]{:S(2)}, u32[]{:S(2)}) collective-permute-start(f32[7,32,256]{2,1,0:T(8,128)S(1)} %get-tuple-element.7), channel_id=1, source_target_pairs={{16,32},{32,16},{48,64},{64,48},{80,96},{96,80},{112,128},{128,112... | collective-permute-start | bytes 688136 | tf_op jit(solution)/shard_map/ppermute | solution.py:380
  21.4 2.9 %collective-permute-start.2 = (f32[7,64,128]{2,1,0:T(8,128)S(1)}, f32[7,64,128]{2,1,0:T(8,128)S(1)}, u32[]{:S(2)}, u32[]{:S(2)}) collective-permute-start(f32[7,64,128]{2,1,0:T(8,128)S(1)} %get-tuple-element.8), channel_id=1, source_target_pairs={{0,1},{1,0},{2,3},{3,2},{4,5},{5,4},{6,7},{7,6},{8,9},{9,8},{10,11... | collective-permute-start | bytes 688136 | tf_op jit(solution)/shard_map/ppermute | solution.py:380
  21.4 9.7 %collective-permute-start.3 = (f32[7,64,128]{2,1,0:T(8,128)S(1)}, f32[7,64,128]{2,1,0:T(8,128)S(1)}, u32[]{:S(2)}, u32[]{:S(2)}) collective-permute-start(f32[7,64,128]{2,1,0:T(8,128)S(1)} %get-tuple-element.9), channel_id=1, source_target_pairs={{1,2},{2,1},{3,4},{4,3},{5,6},{6,5},{7,8},{8,7},{9,10},{10,9},{11,... | collective-permute-start | bytes 688136 | tf_op jit(solution)/shard_map/ppermute | solution.py:380
  24.3 9.8 %copy-start.4 = (f32[7,64,128]{2,1,0:T(8,128)}, f32[7,64,128]{2,1,0:T(8,128)S(1)}, u32[]{:S(2)}) copy-start(f32[7,64,128]{2,1,0:T(8,128)S(1)} %collective-permute-done.2.y0) | copy-start | bytes 688132
  31.1 3.0 %copy-start.5 = (f32[7,64,128]{2,1,0:T(8,128)}, f32[7,64,128]{2,1,0:T(8,128)S(1)}, u32[]{:S(2)}) copy-start(f32[7,64,128]{2,1,0:T(8,128)S(1)} %collective-permute-done.3.y1) | copy-start | bytes 688132
  31.2 7.1 %collective-permute-start.5 = (f32[7,32,128]{2,1,0:T(8,128)S(1)}, f32[7,32,128]{2,1,0:T(8,128)S(1)}, u32[]{:S(2)}, u32[]{:S(2)}) collective-permute-start(f32[7,32,128]{2,1,0:T(8,128)S(1)} %get-tuple-element.10), channel_id=1, source_target_pairs={{16,32},{32,16},{48,64},{64,48},{80,96},{96,80},{112,128},{128,112... | collective-permute-start | bytes 344072 | tf_op jit(solution)/shard_map/ppermute | solution.py:380
  32.6 6.0 %collective-permute-start.4 = (f32[7,32,128]{2,1,0:T(8,128)S(1)}, f32[7,32,128]{2,1,0:T(8,128)S(1)}, u32[]{:S(2)}, u32[]{:S(2)}) collective-permute-start(f32[7,32,128]{2,1,0:T(8,128)S(1)} %get-tuple-element.11), channel_id=1, source_target_pairs={{0,16},{16,0},{32,48},{48,32},{64,80},{80,64},{96,112},{112,96},{1... | collective-permute-start | bytes 344072 | tf_op jit(solution)/shard_map/ppermute | solution.py:380
  34.1 4.5 %copy-start.6 = (f32[7,32,256]{2,1,0:T(8,128)}, f32[7,32,256]{2,1,0:T(8,128)S(1)}, u32[]{:S(2)}) copy-start(f32[7,32,256]{2,1,0:T(8,128)S(1)} %collective-permute-done.x0) | copy-start | bytes 688132
  34.1 4.5 %copy-start.7 = (f32[7,32,256]{2,1,0:T(8,128)}, f32[7,32,256]{2,1,0:T(8,128)S(1)}, u32[]{:S(2)}) copy-start(f32[7,32,256]{2,1,0:T(8,128)S(1)} %collective-permute-done.1.x1) | copy-start | bytes 688132
  38.3 0.6 copy-start.8
  38.9 0.6 copy-start.9

commit v2 on v1

v2 whole, which is shorter than its diff:
```python
import functools

import jax
import jax.numpy as jnp
import numpy as np
from jax import lax
from jax.experimental import pallas as pl
from jax.experimental.pallas import tpu as pltpu
from jax.sharding import PartitionSpec as P

STEPS = 24
NF = 3
RADIUS = 3
COURANT = 0.68

T = 256
PAD = 32
ROWS = T + 2 * PAD
CHUNK = 39
FIRST = (ROWS - 8 * CHUNK) // 2
LANES = 128
DEEP = STEPS + 2
PLANES = 6 * NF
K = 8 * 2 * NF

f32 = jnp.float32
bf16 = jnp.bfloat16


def filter_table():
    offsets = np.arange(-RADIUS, RADIUS + 1)
    dist = np.sqrt(offsets[:, None] ** 2 + offsets[None, :] ** 2)
    table = np.maximum(0.0, RADIUS - dist)
    return table / table.sum()


def lane_iota():
    return lax.broadcasted_iota(jnp.int32, (8, LANES), 1)


def turn(x, shift, axis):
    size = x.shape[axis]
    shift = shift % size
    return x if shift == 0 else pltpu.roll(x, shift, axis)


def right_slot(group, k):
    return 32 * ((group + (2 if k >= 4 else 0)) % 4)


def left_slot(group, k):
    return 32 * ((group + (3 if k >= 4 else 1)) % 4)


def chunked(body, times):
    def several(i, _):
        for u in range(times):
            body(times * i + u)
        return 0

    lax.fori_loop(0, CHUNK // times, several, 0)


def riders(k):
    return [(jj, m) for jj, m in enumerate(range(3 * k, 3 * k + 3)) if m <= PLANES]


def pack_kernel(fields, inv_eps, fwd, mask, xs0, xs1, ys0, ys1, f7, fw, mk, sems):
    even_x = lax.rem(lax.axis_index("gx"), 2) == 0
    even_y = lax.rem(lax.axis_index("gy"), 2) == 0
    loads = [
        pltpu.make_async_copy(fields, f7.at[pl.ds(0, 6)], sems.at[0]),
        pltpu.make_async_copy(inv_eps, f7.at[6], sems.at[1]),
        pltpu.make_async_copy(mask, mk, sems.at[2]),
        pltpu.make_async_copy(fwd, fw.at[pl.ds(0, PLANES)], sems.at[3]),
    ]
    for copy in loads:
        copy.start()
    lane = lane_iota()
    sub = lax.broadcasted_iota(jnp.int32, (8, T), 0)

    def rows(ref, k, g, j, t):
        return ref[k, pl.ds(pl.multiple_of(64 * g + 8 * j, 8), 8), pl.ds(LANES * t, LANES)]

    def main(i, _):
        for j in (2 * i, 2 * i + 1):
            to = pl.ds(pl.multiple_of(8 * j, 8), 8)
            for k in range(7):
                first = last = None
                for g in range(4):
                    a = turn(rows(f7, k, g, j, 0), right_slot(g, k), 1)
                    b = turn(rows(f7, k, g, j, 1), left_slot(g, k) - 96, 1)
                    first = a if g == 0 else jnp.where(lane // 32 == right_slot(g, k) // 32, a, first)
                    last = b if g == 0 else jnp.where(lane // 32 == left_slot(g, k) // 32, b, last)
                ys0[k, to] = first
                ys1[k, to] = last
        return 0

    def ride(i, _):
        for j in (2 * i, 2 * i + 1):
            to = pl.ds(pl.multiple_of(8 * j, 8), 8)
            for k in range(7):
                first, last = ys0[k, to], ys1[k, to]
                for jj, m in riders(k):
                    for g in range(4):
                        a, b = right_slot(g, k) + 26 + 2 * jj, left_slot(g, k) + 2 * jj
                        first = jnp.where(lane // 2 == a // 2, turn(rows(fw, m, g, j, 0), a, 1), first)
                        last = jnp.where(lane // 2 == b // 2, turn(rows(fw, m, g, j, 1), b - 126, 1), last)
                ys0[k, to] = jnp.where(even_y, last, first)
                ys1[k, to] = jnp.where(even_y, first, last)
        return 0

    loads[0].wait()
    loads[1].wait()
    lax.fori_loop(0, 4, main, 0)
    loads[2].wait()
    fw[PLANES] = mk[...].astype(f32)
    loads[3].wait()
    lax.fori_loop(0, 4, ride, 0)
    for k in range(7):
        low, high = f7[k, pl.ds(T - 32, 8)], f7[k, pl.ds(24, 8)]
        for jj, m in riders(k):
            low = jnp.where(sub // 2 == jj, turn(fw[m, pl.ds(T - 8, 8)], 2 * jj + 2, 0), low)
            high = jnp.where(sub // 2 == jj + 1, turn(fw[m, pl.ds(0, 8)], 2 * jj + 2, 0), high)
        for j in range(4):
            a = low if j == 0 else f7[k, pl.ds(T - 32 + 8 * j, 8)]
            b = high if j == 3 else f7[k, pl.ds(8 * j, 8)]
            xs0[k, pl.ds(8 * j, 8)] = jnp.where(even_x, a, b)
            xs1[k, pl.ds(8 * j, 8)] = jnp.where(even_x, b, a)


def pack(fields, inv_eps, fwd, mask):
    x_slab = jax.ShapeDtypeStruct((7, 32, T), f32)
    y_slab = jax.ShapeDtypeStruct((7, 64, LANES), f32)
    return pl.pallas_call(
        pack_kernel,
        out_shape=(x_slab, x_slab, y_slab, y_slab),
        in_specs=[pl.BlockSpec(memory_space=pl.ANY)] * 4,
        out_specs=(pl.BlockSpec(memory_space=pltpu.VMEM),) * 4,
        scratch_shapes=[
            pltpu.VMEM((7, T, T), f32),
            pltpu.VMEM((PLANES + 1, T, T), f32),
            pltpu.VMEM((T, T), jnp.int32),
            pltpu.SemaphoreType.DMA((4,)),
        ],
        compiler_params=pltpu.CompilerParams(vmem_limit_bytes=56 * 2**20),
        name="pack",
    )(fields, inv_eps, fwd, mask)


def next_lane(tiles, lane):
    r = [turn(x, -1, 1) for x in tiles]
    return [jnp.where(lane == LANES - 1, r[(t + 1) % 3], r[t]) for t in range(3)]


def prev_lane(tiles, lane):
    r = [turn(x, 1, 1) for x in tiles]
    return [jnp.where(lane == 0, r[(t + 2) % 3], r[t]) for t in range(3)]


def main_kernel(table, fields, inv_eps, fwd, mask, y0, y1, x0, x1, c0, c1, out, grad,
                stage, fst, mk, yl, yr, cl, ch, coef, e, h, fac, raw, sems):
    px = lax.rem(lax.axis_index("gx"), 2)
    py = lax.rem(lax.axis_index("gy"), 2)
    own = pl.ds(PAD, T)
    copies, late = [], []
    for t in range(2):
        cols = pl.ds(LANES * t, LANES)
        copies.append(pltpu.make_async_copy(fields.at[:, :, cols], stage.at[pl.ds(0, 6), t, own], sems.at[t]))
        copies.append(pltpu.make_async_copy(inv_eps.at[:, cols], stage.at[6, t, own], sems.at[2 + t]))
        late.append(pltpu.make_async_copy(fwd.at[:, :, cols], fst.at[pl.ds(0, PLANES), t, own], sems.at[4 + t]))
    late.append(pltpu.make_async_copy(mask, mk, sems.at[6]))

    for copy in copies + late:
        copy.start()

    row = lax.broadcasted_iota(jnp.int32, (16, 3 * K), 0)
    col = lax.broadcasted_iota(jnp.int32, (16, 3 * K), 1)

    def spread(i, _):
        block = jnp.zeros((16, 3 * K), f32)
        for u in range(2):
            for j in range(6 * NF):
                block = jnp.where((row == col - 8 * j + 8 * u) & (col // 8 == j), table[2 * i + u, j], block)
        coef[pl.ds(pl.multiple_of(16 * i, 16), 16)] = block.astype(bf16)
        return 0

    lax.fori_loop(0, STEPS // 2, spread, 0)

    def deal(even, refs, to_low, to_high):
        @pl.when(even)
        def _():
            to_low(refs[1])
            to_high(refs[0])

        @pl.when(jnp.logical_not(even))
        def _():
            to_low(refs[0])
            to_high(refs[1])

    def into(ref):
        def copy(src):
            ref[...] = src[...]

        return copy

    def rim(row):
        def copy(src):
            for t in range(2):
                stage[:, t, pl.ds(row, PAD)] = src[:, :, pl.ds(LANES * t, LANES)]

        return copy

    deal(px == 0, (x0, x1), rim(0), rim(PAD + T))
    deal(py == 0, (y0, y1), into(yl), into(yr))
    deal(px == 0, (c0, c1), into(cl), into(ch))

    lane = lane_iota()
    sub = lax.broadcasted_iota(jnp.int32, (8, LANES), 0)
    right_half = lane < 64

    def fill(j, _):
        at = pl.ds(pl.multiple_of(8 * j, 8), 8)
        for k in range(7):
            r, l = yr[k, at], yl[k, at]
            for g in range(4):
                to = pl.ds(pl.multiple_of(PAD + 64 * g + 8 * j, 8), 8)
                stage[k, 2, to] = jnp.where(
                    right_half, turn(r, -right_slot(g, k), 1), turn(l, 96 - left_slot(g, k), 1)
                )
                for jj, m in enumerate(range(3 * k, min(3 * k + 3, PLANES + 1))):
                    fst[m, 2, to] = jnp.where(
                        right_half,
                        turn(r, -right_slot(g, k) - 26 - 2 * jj, 1),
                        turn(l, 126 - left_slot(g, k) - 2 * jj, 1),
                    )
        return 0

    lax.fori_loop(0, 8, fill, 0)
    zero = jnp.zeros((8, LANES), f32)
    for k in range(7):
        c = k % 4
        rl, ll, rh, lh = right_slot(3, k), left_slot(3, k), right_slot(0, k), left_slot(0, k)
        for j in range(4):
            a, b = cl[c, pl.ds(8 * j, 8)], ch[c, pl.ds(8 * j, 8)]
            stage[k, 2, pl.ds(8 * j, 8)] = jnp.where(right_half, turn(a, -rl, 1), turn(a, 96 - ll, 1))
            stage[k, 2, pl.ds(PAD + T + 8 * j, 8)] = jnp.where(right_half, turn(b, -rh, 1), turn(b, 96 - lh, 1))
        a, b = cl[c, pl.ds(24, 8)], ch[c, pl.ds(0, 8)]
        for jj, m in riders(k):
            fst[m, 2, pl.ds(24, 8)] = jnp.where(
                right_half, turn(a, -rl - 26 - 2 * jj, 1), turn(a, 126 - ll - 2 * jj, 1)
            )
            fst[m, 2, pl.ds(PAD + T, 8)] = jnp.where(
                right_half, turn(b, -rh - 26 - 2 * jj, 1), turn(b, 126 - lh - 2 * jj, 1)
            )
            for t in range(2):
                lo, hi = stage[k, t, pl.ds(0, 8)], stage[k, t, pl.ds(ROWS - 8, 8)]
                fst[m, t, pl.ds(24, 8)] = jnp.where(sub >= 6, turn(lo, 6 - 2 * jj, 0), 0.0)
                fst[m, t, pl.ds(PAD + T, 8)] = jnp.where(sub < 2, turn(hi, -2 - 2 * jj, 0), 0.0)
            for t in range(3):
                for j in range(3):
                    fst[m, t, pl.ds(8 * j, 8)] = zero
                    fst[m, t, pl.ds(PAD + T + 8 + 8 * j, 8)] = zero

    def lift(v):
        at = pl.ds(FIRST + v, 8, stride=CHUNK)
        for t in range(3):
            for c in range(3):
                e[0, c, v, t] = stage[c, t, at, :]
                h[c, v, t] = stage[3 + c, t, at, :] * (1.0 / COURANT)
            fac[v, t] = stage[6, t, at, :] * (COURANT * COURANT)

    for copy in copies:
        copy.wait()
    chunked(lift, 3)

    def put(ref, tiles, v):
        for t in range(3):
            ref[v, t] = tiles[t]

    def get(ref, v):
        return [ref[v, t] for t in range(3)]

    def step(n, _):
        old, new = e.at[n], e.at[n + 1]
        ey, ez = get(old.at[1], 0), get(old.at[2], 0)
        end = ([turn(x, -1, 0) for x in ey], [turn(x, -1, 0) for x in ez])
        for v in range(CHUNK):
            ey_n, ez_n = (get(old.at[1], v + 1), get(old.at[2], v + 1)) if v < CHUNK - 1 else end
            ex = get(old.at[0], v)
            xn, zn = next_lane(ex, lane), next_lane(ez, lane)
            hx, hy, hz = get(h.at[0], v), get(h.at[1], v), get(h.at[2], v)
            for t in range(3):
                hx[t] = hx[t] - (zn[t] - ez[t])
                hy[t] = hy[t] + (ez_n[t] - ez[t])
                hz[t] = hz[t] - ((ey_n[t] - ey[t]) - (xn[t] - ex[t]))
            put(h.at[0], hx, v)
            put(h.at[1], hy, v)
            put(h.at[2], hz, v)
            ey, ez = ey_n, ez_n
        hy_p, hz_p = [turn(x, 1, 0) for x in hy], [turn(x, 1, 0) for x in hz]
        for v in range(CHUNK):
            hx, hy, hz = get(h.at[0], v), get(h.at[1], v), get(h.at[2], v)
            xp, zp, f = prev_lane(hx, lane), prev_lane(hz, lane), get(fac, v)
            ex, ey, ez = get(old.at[0], v), get(old.at[1], v), get(old.at[2], v)
            for t in range(3):
                ex[t] = ex[t] + f[t] * (hz[t] - zp[t])
                ey[t] = ey[t] - f[t] * (hz[t] - hz_p[t])
                ez[t] = ez[t] + f[t] * ((hy[t] - hy_p[t]) - (hx[t] - xp[t]))
            put(new.at[0], ex, v)
            put(new.at[1], ey, v)
            put(new.at[2], ez, v)
            hy_p, hz_p = hy, hz
        return 0

    lax.fori_loop(0, STEPS // 2, lambda i, _: step(2 * i + 1, step(2 * i, 0)), 0)

    for copy in late:
        copy.wait()
    for t in range(2):
        fst[PLANES, t, own] = mk[:, pl.ds(LANES * t, LANES)].astype(f32)

    def lower(v):
        at = pl.ds(FIRST + v, 8, stride=CHUNK)
        for t in range(2):
            for c in range(3):
                stage[c, t, at, :] = e[STEPS, c, v, t]
                stage[3 + c, t, at, :] = h[c, v, t] * COURANT

    chunked(lower, 3)
    stores = [
        pltpu.make_async_copy(stage.at[pl.ds(0, 6), t, own], out.at[:, :, pl.ds(LANES * t, LANES)], sems.at[t])
        for t in range(2)
    ]
    for copy in stores:
        copy.start()

    def gather(v):
        at = pl.ds(FIRST + v, 8, stride=CHUNK)
        total = [zero] * 3
        for c in range(3):
            w = jnp.concatenate(
                [jnp.concatenate([fst[3 * i + c, t, at, :] for t in range(3)], axis=1) for i in range(2 * NF)], axis=0
            )
            hi = w.astype(bf16)
            lo = (w - hi.astype(f32)).astype(bf16)
            g = jnp.dot(coef[...], jnp.concatenate([hi, hi, lo], axis=0), preferred_element_type=f32)
            for n in range(STEPS):
                for t in range(3):
                    total[t] = total[t] + e[n + 1, c, v, t] * g[8 * n : 8 * n + 8, LANES * t : LANES * t + LANES]
        for t in range(3):
            raw[v + 2, t] = total[t] * fst[PLANES, t, at, :]

    chunked(gather, 13)
    for t in range(3):
        for v in range(2):
            raw[v, t] = turn(raw[CHUNK + v, t], 1, 0)
            raw[CHUNK + 2 + v, t] = turn(raw[2 + v, t], -1, 0)

    taps = filter_table()

    def smooth(v):
        part = []
        for t in range(3):
            r0 = raw[v + 2, t]
            r1 = raw[v + 1, t] + raw[v + 3, t]
            r2 = raw[v, t] + raw[v + 4, t]
            part.append([
                float(taps[3, 3 + b]) * r0 + float(taps[4, 3 + b]) * r1 + float(taps[5, 3 + b]) * r2 for b in range(3)
            ])
        at = pl.ds(FIRST + v, 8, stride=CHUNK)
        for t in range(2):
            acc = part[t][0]
            for b in (1, 2):
                up = jnp.where(lane >= LANES - b, turn(part[(t + 1) % 3][b], -b, 1), turn(part[t][b], -b, 1))
                down = jnp.where(lane < b, turn(part[(t + 2) % 3][b], b, 1), turn(part[t][b], b, 1))
                acc = acc + (up + down)
            stage[6, t, at, :] = acc

    chunked(smooth, 13)
    stores += [
        pltpu.make_async_copy(stage.at[6, t, own], grad.at[:, pl.ds(LANES * t, LANES)], sems.at[2 + t]) for t in range(2)
    ]
    for copy in stores[2:]:
        copy.start()
    for copy in stores:
        copy.wait()


def advance(table, fields, inv_eps, fwd, mask, *edges):
    vmem = pl.BlockSpec(memory_space=pltpu.VMEM)
    any_space = pl.BlockSpec(memory_space=pl.ANY)
    return pl.pallas_call(
        main_kernel,
        out_shape=(jax.ShapeDtypeStruct((6, T, T), f32), jax.ShapeDtypeStruct((T, T), f32)),
        in_specs=[pl.BlockSpec(memory_space=pltpu.SMEM)] + [any_space] * 4 + [vmem] * 6,
        out_specs=(any_space,) * 2,
        scratch_shapes=[
            pltpu.VMEM((7, 3, ROWS, LANES), f32),
            pltpu.VMEM((PLANES + 1, 3, ROWS, LANES), f32),
            pltpu.VMEM((T, T), jnp.int32),
            pltpu.VMEM((7, 64, LANES), f32),
            pltpu.VMEM((7, 64, LANES), f32),
            pltpu.VMEM((4, 32, LANES), f32),
            pltpu.VMEM((4, 32, LANES), f32),
            pltpu.VMEM((2 * STEPS * 4, 3 * K), bf16),
            pltpu.VMEM((STEPS + 1, 3, CHUNK, 3, 8, LANES), f32),
            pltpu.VMEM((3, CHUNK, 3, 8, LANES), f32),
            pltpu.VMEM((CHUNK, 3, 8, LANES), f32),
            pltpu.VMEM((CHUNK + 4, 3, 8, LANES), f32),
            pltpu.SemaphoreType.DMA((7,)),
        ],
        compiler_params=pltpu.CompilerParams(vmem_limit_bytes=58 * 2**20),
        name="advance",
    )(table, fields, inv_eps, fwd, mask, *edges)


def swap(x, axis, offset):
    count = lax.axis_size(axis)
    route = []
    for i in range(offset, count + offset, 2):
        a, b = i % count, (i + 1) % count
        route += [(a, b), (b, a)]
    return lax.ppermute(x, axis, route)


def coefficients(phase_start, omega):
    theta = phase_start[None] + omega[None] * jnp.arange(STEPS, dtype=f32)[:, None]
    table = jnp.stack([jnp.cos(theta), -jnp.sin(theta)], axis=2).reshape(STEPS, 2 * NF) / STEPS
    high = lax.reduce_precision(table, 8, 7)
    low = lax.reduce_precision(table - high, 8, 7)
    return jnp.concatenate([high, low, high], axis=1)


def local(fields, inv_eps, fwd_dft, phase_start, omega, mask):
    fwd = fwd_dft.reshape(PLANES, T, T)
    table = coefficients(phase_start, omega)
    xs0, xs1, ys0, ys1 = pack(fields, inv_eps, fwd, mask)
    y0 = swap(ys0, "gy", 0)
    y1 = swap(ys1, "gy", 1)
    x0 = swap(xs0, "gx", 0)
    x1 = swap(xs1, "gx", 1)
    even_x = lax.rem(lax.axis_index("gx"), 2) == 0
    even_y = lax.rem(lax.axis_index("gy"), 2) == 0
    right = jnp.where(even_y, y0, y1)
    left = jnp.where(even_y, y1, y0)
    lane = lax.broadcasted_iota(jnp.int32, (4, 32, LANES), 2)

    def corner(rows, group):
        r, l = right[:, rows], left[:, rows]
        r4, l4 = jnp.concatenate([r[4:], r[:1]]), jnp.concatenate([l[4:], l[:1]])
        block = lane // 32 * 32
        res = jnp.where(block == right_slot(group, 0), r[:4], l[:4])
        res = jnp.where(block == right_slot(group, 4), r4, res)
        return jnp.where(block == left_slot(group, 4), l4, res)

    up, down = corner(slice(32, 64), 3), corner(slice(0, 32), 0)
    c0 = swap(jnp.where(even_x, up, down), "gx", 0)
    c1 = swap(jnp.where(even_x, down, up), "gx", 1)
    return advance(table, fields, inv_eps, fwd, mask, y0, y1, x0, x1, c0, c1)


def solution(mesh):
    return jax.shard_map(
        local,
        mesh=mesh,
        in_specs=(
            P(None, "gx", "gy"),
            P("gx", "gy"),
            P(None, None, None, "gx", "gy"),
            P(),
            P(),
            P("gx", "gy"),
        ),
        out_specs=(P(None, "gx", "gy"), P("gx", "gy")),
        check_vma=False,
    )
```

time: 120 us -> 57.6 us (0.48)
  Pallas kernels: 87.8 us -> 34.6 us
  waiting for transfers between devices: 11.2 us -> 2.05 us
  local copies, waits for them, and re-layouts: 7.93 us -> 0.84 us
  starting transfers between devices: 11.4 us -> 18.3 us
    pallas_call x1, Pallas kernels: 80.1 us -> 29.1 us  [advance(): pl.pallas_call(main_kernel, out_shape=(jax.ShapeDtypeStruct((6, T, T), f3...]
    ppermute x6, waiting for transfers between devices: 11.2 us -> 2.05 us  [swap(): return lax.ppermute(x, axis, route)]
    ppermute x6, starting transfers between devices: 11.4 us -> 18.3 us  [swap(): return lax.ppermute(x, axis, route)]
    unnamed x24 -> x16, local copies, waits for them, and re-layouts: 6.63 us -> 0.64 us
    pallas_call x1, Pallas kernels: 7.74 us -> 5.5 us  [pack(): pl.pallas_call(pack_kernel, out_shape=(x_slab, x_slab, y_slab, y_slab), i...]
    convert_element_type x2 -> x0, local copies, waits for them, and re-layouts: 1.29 us -> none  [coefficients(): return wide.reshape(STEPS * 8, 3 * K).astype(bf16)]
  transfers between devices with their start and end apart: 6 -> 6, of which waited for: 3 -> 2; matrix products, arithmetic and copies ran while one was open for 1% -> 2% of each run, Pallas kernels for 0% -> 0%
where the time goes in v2:
time: 57.6 us; the launch traced here: 57.5 us
  Pallas kernels  34.6 us (60%)
  starting transfers between devices  18.3 us (32%)
  waiting for transfers between devices  2.05 us (4%)
  other arithmetic  0.93 us (2%)
  local copies, waits for them, and re-layouts  0.84 us (1%)
  between operations  0.81 us (1%)
    pallas_call x1, Pallas kernels, advance(): pl.pallas_call(main_kernel, out_shape=(jax.ShapeDtypeStruct((6, T, T), f3...  29.1 us
    ppermute x6, starting transfers between devices, swap(): return lax.ppermute(x, axis, route)  18.3 us
    pallas_call x1, Pallas kernels, pack(): pl.pallas_call(pack_kernel, out_shape=(x_slab, x_slab, y_slab, y_slab), i...  5.5 us
    ppermute x6, waiting for transfers between devices, swap(): return lax.ppermute(x, axis, route)  2.05 us
  transfers between devices with their start and end apart: 6, of which 2 were waited for; matrix products, arithmetic and copies ran while one was open for 2% of the time, Pallas kernels for 0%

profile of v2, /device:TPU:16, one launch (start us, length us, event | category | flops | bytes accessed | tf_op | source)
XLA Modules:
  0.0 57.5 jit_solution(18411176293339756178)
XLA Ops:
  0.6 0.0 copy-start.6
  0.6 0.0 copy-start.7
  0.6 5.5 %pack.1 = (f32[7,32,256]{2,1,0:T(8,128)}, f32[7,32,256]{2,1,0:T(8,128)}, f32[7,64,128]{2,1,0:T(8,128)}, f32[7,64,128]{2,1,0:T(8,128)}) custom-call(f32[6,256,256]{2,1,0:T(8,128)} %fields.3, f32[256,256]{1,0:T(8,128)} %inv_eps.3, f32[18,256,256]{2,1,0:T(8,128)} %bitcast.3, s32[256,256]{1,0:T(8,128)} %mask.3), custom_call_target="tpu_custom_call" | custom-call | tf_op jit(solution)/shard_map/pack/pallas_call | solution.py:135
  6.2 0.1 collective-permute-start
  6.3 2.6 %collective-permute-start.1 = (f32[7,64,128]{2,1,0:T(8,128)}, f32[7,64,128]{2,1,0:T(8,128)S(1)}, u32[]{:S(2)}, u32[]{:S(2)}) collective-permute-start(f32[7,64,128]{2,1,0:T(8,128)} %get-tuple-element.7), channel_id=1, source_target_pairs={{1,2},{2,1},{3,4},{4,3},{5,6},{6,5},{7,8},{8,7},{9,10},{10,9},{11,... | collective-permute-start | bytes 688136 | tf_op jit(solution)/shard_map/ppermute | solution.py:424
  8.9 2.2 %collective-permute-start.2 = (f32[7,32,256]{2,1,0:T(8,128)}, f32[7,32,256]{2,1,0:T(8,128)S(1)}, u32[]{:S(2)}, u32[]{:S(2)}) collective-permute-start(f32[7,32,256]{2,1,0:T(8,128)} %get-tuple-element.8), channel_id=1, source_target_pairs={{0,16},{16,0},{32,48},{48,32},{64,80},{80,64},{96,112},{112,96},{1... | collective-permute-start | bytes 688136 | tf_op jit(solution)/shard_map/ppermute | solution.py:424
  11.1 5.3 %collective-permute-start.3 = (f32[7,32,256]{2,1,0:T(8,128)}, f32[7,32,256]{2,1,0:T(8,128)S(1)}, u32[]{:S(2)}, u32[]{:S(2)}) collective-permute-start(f32[7,32,256]{2,1,0:T(8,128)} %get-tuple-element.9), channel_id=1, source_target_pairs={{16,32},{32,16},{48,64},{64,48},{80,96},{96,80},{112,128},{128,112... | collective-permute-start | bytes 688136 | tf_op jit(solution)/shard_map/ppermute | solution.py:424
  16.4 0.0 copy-done.6
  16.4 0.0 copy-done.7
  16.4 0.1 fusion.8
  16.6 0.1 copy.10
  16.7 0.1 copy.12
  16.8 0.0 collective-permute-done.y0
  16.8 0.0 copy-start
  16.8 0.5 collective-permute-done.1.y1
  17.3 0.0 copy-start.1
  17.4 0.1 collective-permute-start.4
  17.5 8.0 %collective-permute-start.5 = (f32[4,32,128]{2,1,0:T(8,128)S(1)}, f32[4,32,128]{2,1,0:T(8,128)S(1)}, u32[]{:S(2)}, u32[]{:S(2)}) collective-permute-start(f32[4,32,128]{2,1,0:T(8,128)S(1)} %get-tuple-element.10), channel_id=1, source_target_pairs={{16,32},{32,16},{48,64},{64,48},{80,96},{96,80},{112,128},{128,112... | collective-permute-start | bytes 196616 | tf_op jit(solution)/shard_map/ppermute | solution.py:424
  25.5 0.7 %pad_maximum_fusion.table = f32[24,18]{1,0:T(8,128)} fusion(f32[24,6]{1,0:T(8,128)S(1)} %copy.12, f32[24,6]{1,0:T(8,128)S(1)} %subtract_reduce-precision_fusion), kind=kLoop, calls=%fused_computation.15 | loop fusion | flops 864 | bytes 2880 | tf_op jit(solution)/shard_map/concatenate | solution.py:432
  26.2 0.0 collective-permute-done.2.x0
  26.2 0.0 copy-start.2
  26.2 0.0 collective-permute-done.3.x1
  26.2 0.0 copy-start.3
  26.2 0.0 collective-permute-done.4.c0
  26.2 0.0 copy-start.4
  26.2 1.5 %collective-permute-done.5.c1 = f32[4,32,128]{2,1,0:T(8,128)S(1)} collective-permute-done((f32[4,32,128]{2,1,0:T(8,128)S(1)}, f32[4,32,128]{2,1,0:T(8,128)S(1)}, u32[]{:S(2)}, u32[]{:S(2)}) %collective-permute-start.5) | collective-permute-done | bytes 65568 | tf_op jit(solution)/shard_map/ppermute | solution.py:424
  27.7 0.0 copy-done
  27.8 0.0 copy-done.1
  27.8 0.0 copy-done.2
  27.8 0.0 copy-done.3
  27.8 0.0 copy-done.4
  27.8 0.0 copy-start.5
  27.8 0.6 %copy-done.5 = f32[4,32,128]{2,1,0:T(8,128)} copy-done((f32[4,32,128]{2,1,0:T(8,128)}, f32[4,32,128]{2,1,0:T(8,128)S(1)}, u32[]{:S(2)}) %copy-start.5) | copy-done | bytes 65560
  28.4 29.1 %advance.1 = (f32[6,256,256]{2,1,0:T(8,128)}, f32[256,256]{1,0:T(8,128)}) custom-call(f32[24,18]{1,0:T(8,128)} %pad_maximum_fusion.table, f32[6,256,256]{2,1,0:T(8,128)} %fields.3, f32[256,256]{1,0:T(8,128)} %inv_eps.3, f32[18,256,256]{2,1,0:T(8,128)} %bitcast.4, s32[256,256]{1,0:T(8,128)} %mask.3, f32[7,64,128]{2,1,0:T(8,128)} %copy-done, ...), custom_call_target="tpu_custom_call" | custom-call | tf_op jit(solution)/shard_map/advance/pallas_call | solution.py:393
  (11 shorter events, 0.2 us)
Async XLA Ops:
  0.6 15.7 %copy-start.6 = (f32[3]{0:T(128)S(1)}, f32[3]{0:T(128)}, u32[]{:S(2)}) copy-start(f32[3]{0:T(128)} %param.10) | copy-start | bytes 40
  0.6 15.7 %copy-start.7 = (f32[3]{0:T(128)S(1)}, f32[3]{0:T(128)}, u32[]{:S(2)}) copy-start(f32[3]{0:T(128)} %param.9) | copy-start | bytes 40
  6.2 10.6 %collective-permute-start = (f32[7,64,128]{2,1,0:T(8,128)}, f32[7,64,128]{2,1,0:T(8,128)S(1)}, u32[]{:S(2)}, u32[]{:S(2)}) collective-permute-start(f32[7,64,128]{2,1,0:T(8,128)} %get-tuple-element.6), channel_id=1, source_target_pairs={{0,1},{1,0},{2,3},{3,2},{4,5},{5,4},{6,7},{7,6},{8,9},{9,8},{10,11... | collective-permute-start | bytes 688136 | tf_op jit(solution)/shard_map/ppermute | solution.py:424
  6.3 11.0 %collective-permute-start.1 = (f32[7,64,128]{2,1,0:T(8,128)}, f32[7,64,128]{2,1,0:T(8,128)S(1)}, u32[]{:S(2)}, u32[]{:S(2)}) collective-permute-start(f32[7,64,128]{2,1,0:T(8,128)} %get-tuple-element.7), channel_id=1, source_target_pairs={{1,2},{2,1},{3,4},{4,3},{5,6},{6,5},{7,8},{8,7},{9,10},{10,9},{11,... | collective-permute-start | bytes 688136 | tf_op jit(solution)/shard_map/ppermute | solution.py:424
  8.9 17.3 %collective-permute-start.2 = (f32[7,32,256]{2,1,0:T(8,128)}, f32[7,32,256]{2,1,0:T(8,128)S(1)}, u32[]{:S(2)}, u32[]{:S(2)}) collective-permute-start(f32[7,32,256]{2,1,0:T(8,128)} %get-tuple-element.8), channel_id=1, source_target_pairs={{0,16},{16,0},{32,48},{48,32},{64,80},{80,64},{96,112},{112,96},{1... | collective-permute-start | bytes 688136 | tf_op jit(solution)/shard_map/ppermute | solution.py:424
  11.1 15.1 %collective-permute-start.3 = (f32[7,32,256]{2,1,0:T(8,128)}, f32[7,32,256]{2,1,0:T(8,128)S(1)}, u32[]{:S(2)}, u32[]{:S(2)}) collective-permute-start(f32[7,32,256]{2,1,0:T(8,128)} %get-tuple-element.9), channel_id=1, source_target_pairs={{16,32},{32,16},{48,64},{64,48},{80,96},{96,80},{112,128},{128,112... | collective-permute-start | bytes 688136 | tf_op jit(solution)/shard_map/ppermute | solution.py:424
  16.8 11.0 %copy-start = (f32[7,64,128]{2,1,0:T(8,128)}, f32[7,64,128]{2,1,0:T(8,128)S(1)}, u32[]{:S(2)}) copy-start(f32[7,64,128]{2,1,0:T(8,128)S(1)} %collective-permute-done.y0) | copy-start | bytes 688132
  17.3 10.5 %copy-start.1 = (f32[7,64,128]{2,1,0:T(8,128)}, f32[7,64,128]{2,1,0:T(8,128)S(1)}, u32[]{:S(2)}) copy-start(f32[7,64,128]{2,1,0:T(8,128)S(1)} %collective-permute-done.1.y1) | copy-start | bytes 688132
  17.4 8.8 %collective-permute-start.4 = (f32[4,32,128]{2,1,0:T(8,128)S(1)}, f32[4,32,128]{2,1,0:T(8,128)S(1)}, u32[]{:S(2)}, u32[]{:S(2)}) collective-permute-start(f32[4,32,128]{2,1,0:T(8,128)S(1)} %broadcast_select_fusion.3), channel_id=1, source_target_pairs={{0,16},{16,0},{32,48},{48,32},{64,80},{80,64},{96,112},{112,96},{1... | collective-permute-start | bytes 196616 | tf_op jit(solution)/shard_map/ppermute | solution.py:424
  17.5 10.2 %collective-permute-start.5 = (f32[4,32,128]{2,1,0:T(8,128)S(1)}, f32[4,32,128]{2,1,0:T(8,128)S(1)}, u32[]{:S(2)}, u32[]{:S(2)}) collective-permute-start(f32[4,32,128]{2,1,0:T(8,128)S(1)} %get-tuple-element.10), channel_id=1, source_target_pairs={{16,32},{32,16},{48,64},{64,48},{80,96},{96,80},{112,128},{128,112... | collective-permute-start | bytes 196616 | tf_op jit(solution)/shard_map/ppermute | solution.py:424
  26.2 1.6 %copy-start.2 = (f32[7,32,256]{2,1,0:T(8,128)}, f32[7,32,256]{2,1,0:T(8,128)S(1)}, u32[]{:S(2)}) copy-start(f32[7,32,256]{2,1,0:T(8,128)S(1)} %collective-permute-done.2.x0) | copy-start | bytes 688132
  26.2 1.6 %copy-start.3 = (f32[7,32,256]{2,1,0:T(8,128)}, f32[7,32,256]{2,1,0:T(8,128)S(1)}, u32[]{:S(2)}) copy-start(f32[7,32,256]{2,1,0:T(8,128)S(1)} %collective-permute-done.3.x1) | copy-start | bytes 688132
  26.2 1.6 %copy-start.4 = (f32[4,32,128]{2,1,0:T(8,128)}, f32[4,32,128]{2,1,0:T(8,128)S(1)}, u32[]{:S(2)}) copy-start(f32[4,32,128]{2,1,0:T(8,128)S(1)} %collective-permute-done.4.c0) | copy-start | bytes 196612
  27.8 0.6 %copy-start.5 = (f32[4,32,128]{2,1,0:T(8,128)}, f32[4,32,128]{2,1,0:T(8,128)S(1)}, u32[]{:S(2)}) copy-start(f32[4,32,128]{2,1,0:T(8,128)S(1)} %collective-permute-done.5.c1) | copy-start | bytes 196612

commit v3 on v2

v3 whole, which is shorter than its diff:
```python
import functools

import jax
import jax.numpy as jnp
import numpy as np
from jax import lax
from jax.experimental import pallas as pl
from jax.experimental.pallas import tpu as pltpu
from jax.sharding import PartitionSpec as P

STEPS = 24
NF = 3
RADIUS = 3
COURANT = 0.68

T = 256
PAD = 32
ROWS = T + 2 * PAD
CHUNK = ROWS // 8
HALF = CHUNK // 2
LANES = 128
UNROLL = 6
PLANES = 6 * NF
K = 8 * 2 * NF

f32 = jnp.float32
bf16 = jnp.bfloat16


def filter_table():
    offsets = np.arange(-RADIUS, RADIUS + 1)
    dist = np.sqrt(offsets[:, None] ** 2 + offsets[None, :] ** 2)
    table = np.maximum(0.0, RADIUS - dist)
    return table / table.sum()


def lane_iota():
    return lax.broadcasted_iota(jnp.int32, (8, LANES), 1)


def turn(x, shift, axis):
    size = x.shape[axis]
    shift = shift % size
    return x if shift == 0 else pltpu.roll(x, shift, axis)


def right_slot(group, k):
    return 32 * ((group + (2 if k >= 4 else 0)) % 4)


def left_slot(group, k):
    return 32 * ((group + (3 if k >= 4 else 1)) % 4)


def chunked(body, times):
    def several(i, _):
        for u in range(times):
            body(times * i + u)
        return 0

    lax.fori_loop(0, HALF // times, several, 0)


def riders(k):
    return [(jj, m) for jj, m in enumerate(range(3 * k, 3 * k + 3)) if m <= PLANES]


def x_slab(side, plane, rider, write):
    sub = lax.broadcasted_iota(jnp.int32, (8, T), 0)
    for k in range(7):
        edge = plane(k, 0 if side == 0 else 24)
        for jj, m in riders(k):
            edge = jnp.where(sub // 2 == jj + side, turn(rider(m), 2 * jj + 2, 0), edge)
        for j in range(4):
            write(k, 8 * j, edge if j == 3 * side else plane(k, 8 * j))


def pack_kernel(fields, inv_eps, fwd, mask, xs0, xs1, ys0, ys1, f7, fw, mk, sems):
    even_x = lax.rem(lax.axis_index("gx"), 2) == 0
    even_y = lax.rem(lax.axis_index("gy"), 2) == 0
    loads = [
        pltpu.make_async_copy(fields, f7.at[pl.ds(0, 6)], sems.at[0]),
        pltpu.make_async_copy(inv_eps, f7.at[6], sems.at[1]),
        pltpu.make_async_copy(mask, mk, sems.at[2]),
    ]
    loads += [
        pltpu.make_async_copy(fwd.at[pl.ds(3 * k, 3)], fw.at[pl.ds(3 * k, 3)], sems.at[3 + k]) for k in range(6)
    ]
    for copy in loads:
        copy.start()
    lane = lane_iota()

    def rows(ref, k, g, j, t):
        return ref[k, pl.ds(64 * g + 8 * j, 8), pl.ds(LANES * t, LANES)]

    loads[0].wait()
    loads[1].wait()
    for k in (6, 0, 1, 2, 3, 4, 5):
        if k == 6:
            loads[2].wait()
            fw[PLANES] = mk[...].astype(f32)
        else:
            loads[3 + k].wait()
        for j in range(8):
            first = last = None
            for g in range(4):
                a = turn(rows(f7, k, g, j, 0), right_slot(g, k), 1)
                b = turn(rows(f7, k, g, j, 1), left_slot(g, k) - 96, 1)
                first = a if g == 0 else jnp.where(lane // 32 == right_slot(g, k) // 32, a, first)
                last = b if g == 0 else jnp.where(lane // 32 == left_slot(g, k) // 32, b, last)
            for jj, m in riders(k):
                for g in range(4):
                    a, b = right_slot(g, k) + 26 + 2 * jj, left_slot(g, k) + 2 * jj
                    first = jnp.where(lane // 2 == a // 2, turn(rows(fw, m, g, j, 0), a, 1), first)
                    last = jnp.where(lane // 2 == b // 2, turn(rows(fw, m, g, j, 1), b - 126, 1), last)
            to = pl.ds(8 * j, 8)
            ys0[k, to] = jnp.where(even_y, last, first)
            ys1[k, to] = jnp.where(even_y, first, last)

    def write(side):
        def put_row(k, row, value):
            if side == 0:
                xs0[k, pl.ds(row, 8)] = value
            else:
                xs1[k, pl.ds(row, 8)] = value

        return put_row

    for flip, here in ((0, even_x), (1, jnp.logical_not(even_x))):
        @pl.when(here)
        def _():
            for side, (base, near) in enumerate(((T - 32, T - 8), (0, 0))):
                x_slab(
                    side,
                    lambda k, row: f7[k, pl.ds(base + row, 8)],
                    lambda m: fw[m, pl.ds(near, 8)],
                    write(side ^ flip),
                )


def pack(fields, inv_eps, fwd, mask):
    x_shape = jax.ShapeDtypeStruct((7, 32, T), f32)
    y_shape = jax.ShapeDtypeStruct((7, 64, LANES), f32)
    return pl.pallas_call(
        pack_kernel,
        out_shape=(x_shape, x_shape, y_shape, y_shape),
        in_specs=[pl.BlockSpec(memory_space=pl.ANY)] * 4,
        out_specs=(pl.BlockSpec(memory_space=pltpu.VMEM),) * 4,
        scratch_shapes=[
            pltpu.VMEM((7, T, T), f32),
            pltpu.VMEM((PLANES + 1, T, T), f32),
            pltpu.VMEM((T, T), jnp.int32),
            pltpu.SemaphoreType.DMA((9,)),
        ],
        compiler_params=pltpu.CompilerParams(vmem_limit_bytes=56 * 2**20),
        cost_estimate=pl.CostEstimate(flops=10**7, bytes_accessed=7 * 10**6, transcendentals=0),
        name="pack",
    )(fields, inv_eps, fwd, mask)


def half_turn(x):
    return turn(x, LANES // 2, 1)


def next_lane(q, lane, by=1):
    a0, a1, b0, b1, x = [turn(z, -by, 1) for z in q]
    end, mid = lane >= LANES - by, (lane >= 64 - by) & (lane < 64)
    return [
        jnp.where(end, a1, a0),
        jnp.where(end, x, a1),
        jnp.where(mid, b1, b0),
        jnp.where(mid, x, b1),
        jnp.where(end, a0, jnp.where(mid, b0, x)),
    ]


def prev_lane(q, lane, by=1):
    a0, a1, b0, b1, x = [turn(z, by, 1) for z in q]
    end, mid = lane < by, (lane >= 64) & (lane < 64 + by)
    return [
        jnp.where(end, x, a0),
        jnp.where(end, a0, a1),
        jnp.where(mid, x, b0),
        jnp.where(mid, b0, b1),
        jnp.where(end, a1, jnp.where(mid, b1, x)),
    ]


def of_first(lane):
    return (lane < 32) | (lane >= 96)


def wrap_next(q, lane):
    a0, a1, b0, b1, x = [half_turn(z) for z in q]
    return [b0, b1, turn(a0, -1, 0), turn(a1, -1, 0), jnp.where(of_first(lane), x, turn(x, -1, 0))]


def wrap_prev(q, lane):
    a0, a1, b0, b1, x = [half_turn(z) for z in q]
    return [turn(b0, 1, 0), turn(b1, 1, 0), a0, a1, jnp.where(of_first(lane), turn(x, 1, 0), x)]


def load_pair(plane, u, lane):
    v, w = pl.ds(u, 8, stride=CHUNK), pl.ds(u + HALF, 8, stride=CHUNK)
    res = [plane(t)[v, :] for t in range(2)] + [half_turn(plane(t)[w, :]) for t in range(2)]
    return res + [jnp.where(of_first(lane), plane(2)[v, :], half_turn(plane(2)[w, :]))]


def store_pair(plane, u, q):
    v, w = pl.ds(u, 8, stride=CHUNK), pl.ds(u + HALF, 8, stride=CHUNK)
    for t in range(2):
        plane(t)[v, :] = q[t]
        plane(t)[w, :] = half_turn(q[2 + t])


def main_kernel(table, fields, inv_eps, fwd, mask, y0, y1, x0, x1, c0, c1, out, grad,
                stage, fst, mk, yl, yr, cl, ch, coef, e, h, fac, raw, sems):
    px = lax.rem(lax.axis_index("gx"), 2)
    py = lax.rem(lax.axis_index("gy"), 2)
    own = pl.ds(PAD, T)
    copies, late = [], []
    for t in range(2):
        cols = pl.ds(LANES * t, LANES)
        copies.append(pltpu.make_async_copy(fields.at[:, :, cols], stage.at[pl.ds(0, 6), t, own], sems.at[t]))
        copies.append(pltpu.make_async_copy(inv_eps.at[:, cols], stage.at[6, t, own], sems.at[2 + t]))
        late.append(pltpu.make_async_copy(fwd.at[:, :, cols], fst.at[pl.ds(0, PLANES), t, own], sems.at[4 + t]))
    late.append(pltpu.make_async_copy(mask, mk, sems.at[6]))

    def edges(low, high, left, right, clow, chigh):
        res = []
        for t in range(2):
            cols = pl.ds(LANES * t, LANES)
            res.append(pltpu.make_async_copy(low.at[:, :, cols], stage.at[:, t, pl.ds(0, PAD)], sems.at[7 + t]))
            res.append(pltpu.make_async_copy(high.at[:, :, cols], stage.at[:, t, pl.ds(PAD + T, PAD)], sems.at[9 + t]))
        res.append(pltpu.make_async_copy(left, yl, sems.at[11]))
        res.append(pltpu.make_async_copy(right, yr, sems.at[12]))
        res.append(pltpu.make_async_copy(clow, cl, sems.at[13]))
        res.append(pltpu.make_async_copy(chigh, ch, sems.at[14]))
        return res

    for ix in range(2):
        for iy in range(2):
            @pl.when((px == ix) & (py == iy))
            def _():
                xs = (x1, x0) if ix == 0 else (x0, x1)
                ys = (y1, y0) if iy == 0 else (y0, y1)
                cs = (c1, c0) if ix == 0 else (c0, c1)
                for copy in edges(*xs, *ys, *cs):
                    copy.start()
    for copy in copies + late:
        copy.start()

    row = lax.broadcasted_iota(jnp.int32, (16, 3 * K), 0)
    col = lax.broadcasted_iota(jnp.int32, (16, 3 * K), 1)

    def spread(i, _):
        block = jnp.zeros((16, 3 * K), f32)
        for u in range(2):
            for j in range(6 * NF):
                block = jnp.where((row == col - 8 * j + 8 * u) & (col // 8 == j), table[2 * i + u, j], block)
        coef[pl.ds(pl.multiple_of(16 * i, 16), 16)] = block.astype(bf16)
        return 0

    lax.fori_loop(0, STEPS // 2, spread, 0)

    for copy in edges(x0, x1, y0, y1, c0, c1):
        copy.wait()

    lane = lane_iota()
    sub = lax.broadcasted_iota(jnp.int32, (8, LANES), 0)
    right_half = lane < 64

    def fill(j, _):
        at = pl.ds(pl.multiple_of(8 * j, 8), 8)
        for k in range(7):
            r, l = yr[k, at], yl[k, at]
            for g in range(4):
                to = pl.ds(pl.multiple_of(PAD + 64 * g + 8 * j, 8), 8)
                stage[k, 2, to] = jnp.where(
                    right_half, turn(r, -right_slot(g, k), 1), turn(l, 96 - left_slot(g, k), 1)
                )
                for jj, m in enumerate(range(3 * k, min(3 * k + 3, PLANES + 1))):
                    fst[m, 2, to] = jnp.where(
                        right_half,
                        turn(r, -right_slot(g, k) - 26 - 2 * jj, 1),
                        turn(l, 126 - left_slot(g, k) - 2 * jj, 1),
                    )
        return 0

    lax.fori_loop(0, 8, fill, 0)
    zero = jnp.zeros((8, LANES), f32)
    for k in range(7):
        c = k % 4
        rl, ll, rh, lh = right_slot(3, k), left_slot(3, k), right_slot(0, k), left_slot(0, k)
        for j in range(4):
            a, b = cl[c, pl.ds(8 * j, 8)], ch[c, pl.ds(8 * j, 8)]
            stage[k, 2, pl.ds(8 * j, 8)] = jnp.where(right_half, turn(a, -rl, 1), turn(a, 96 - ll, 1))
            stage[k, 2, pl.ds(PAD + T + 8 * j, 8)] = jnp.where(right_half, turn(b, -rh, 1), turn(b, 96 - lh, 1))
        a, b = cl[c, pl.ds(24, 8)], ch[c, pl.ds(0, 8)]
        for jj, m in riders(k):
            fst[m, 2, pl.ds(24, 8)] = jnp.where(
                right_half, turn(a, -rl - 26 - 2 * jj, 1), turn(a, 126 - ll - 2 * jj, 1)
            )
            fst[m, 2, pl.ds(PAD + T, 8)] = jnp.where(
                right_half, turn(b, -rh - 26 - 2 * jj, 1), turn(b, 126 - lh - 2 * jj, 1)
            )
            for t in range(2):
                lo, hi = stage[k, t, pl.ds(0, 8)], stage[k, t, pl.ds(ROWS - 8, 8)]
                fst[m, t, pl.ds(24, 8)] = jnp.where(sub >= 6, turn(lo, 6 - 2 * jj, 0), 0.0)
                fst[m, t, pl.ds(PAD + T, 8)] = jnp.where(sub < 2, turn(hi, -2 - 2 * jj, 0), 0.0)
            for t in range(3):
                for j in range(3):
                    fst[m, t, pl.ds(8 * j, 8)] = zero
                    fst[m, t, pl.ds(PAD + T + 8 + 8 * j, 8)] = zero

    def staged(ref, k):
        return lambda t: ref.at[k, t]

    def put(ref, q, u):
        for i in range(5):
            ref[u, i] = q[i]

    def get(ref, u):
        return [ref[u, i] for i in range(5)]

    def lift(u):
        for c in range(3):
            put(e.at[0, c], load_pair(staged(stage, c), u, lane), u)
            put(h.at[c], [z * (1.0 / COURANT) for z in load_pair(staged(stage, 3 + c), u, lane)], u)
        put(fac, [z * (COURANT * COURANT) for z in load_pair(staged(stage, 6), u, lane)], u)

    for copy in copies:
        copy.wait()
    chunked(lift, 10)

    def step(n, first):
        old, new = e.at[n], e.at[n + 1]

        def after(c, u):
            return get(old.at[c], u + 1) if u < HALF - 1 else wrap_next(get(old.at[c], 0), lane)

        ey, ez = get(old.at[1], first), get(old.at[2], first)
        for k in range(HALF):
            u = (first + k) % HALF
            if u == 0 and k > 0:
                ey, ez = get(old.at[1], 0), get(old.at[2], 0)
            ex, ey_n, ez_n = get(old.at[0], u), after(1, u), after(2, u)
            xn, zn = next_lane(ex, lane), next_lane(ez, lane)
            hx, hy, hz = get(h.at[0], u), get(h.at[1], u), get(h.at[2], u)
            for i in range(5):
                hx[i] = hx[i] - (zn[i] - ez[i])
                hy[i] = hy[i] + (ez_n[i] - ez[i])
                hz[i] = hz[i] - ((ey_n[i] - ey[i]) - (xn[i] - ex[i]))
            put(h.at[0], hx, u)
            put(h.at[1], hy, u)
            put(h.at[2], hz, u)
            ey, ez = ey_n, ez_n
        hy_p, hz_p = get(h.at[1], first), get(h.at[2], first)
        for k in range(HALF):
            u = (first + 1 + k) % HALF
            if u == 0:
                hy_p, hz_p = wrap_prev(hy_p, lane), wrap_prev(hz_p, lane)
            hx, hy, hz = get(h.at[0], u), get(h.at[1], u), get(h.at[2], u)
            xp, zp, f = prev_lane(hx, lane), prev_lane(hz, lane), get(fac, u)
            ex, ey, ez = get(old.at[0], u), get(old.at[1], u), get(old.at[2], u)
            for i in range(5):
                ex[i] = ex[i] + f[i] * (hz[i] - zp[i])
                ey[i] = ey[i] - f[i] * (hz[i] - hz_p[i])
                ez[i] = ez[i] + f[i] * ((hy[i] - hy_p[i]) - (hx[i] - xp[i]))
            put(new.at[0], ex, u)
            put(new.at[1], ey, u)
            put(new.at[2], ez, u)
            hy_p, hz_p = hy, hz

    def steps(i, _):
        for k in range(UNROLL):
            step(UNROLL * i + k, k)
        return 0

    lax.fori_loop(0, STEPS // UNROLL, steps, 0)

    for copy in late:
        copy.wait()
    for t in range(2):
        fst[PLANES, t, own] = mk[:, pl.ds(LANES * t, LANES)].astype(f32)

    def lower(u):
        for c in range(3):
            store_pair(staged(stage, c), u, get(e.at[STEPS, c], u))
            store_pair(staged(stage, 3 + c), u, [z * COURANT for z in get(h.at[c], u)])

    chunked(lower, 10)
    stores = [
        pltpu.make_async_copy(stage.at[pl.ds(0, 6), t, own], out.at[:, :, pl.ds(LANES * t, LANES)], sems.at[t])
        for t in range(2)
    ]
    for copy in stores:
        copy.start()

    def gather(u):
        total = [zero] * 5
        for c in range(3):
            w = jnp.concatenate(
                [jnp.concatenate(load_pair(staged(fst, 3 * i + c), u, lane), axis=1) for i in range(2 * NF)], axis=0
            )
            hi = w.astype(bf16)
            lo = (w - hi.astype(f32)).astype(bf16)
            g = jnp.dot(coef[...], jnp.concatenate([hi, hi, lo], axis=0), preferred_element_type=f32)
            for n in range(STEPS):
                for i in range(5):
                    total[i] = total[i] + e[n + 1, c, u, i] * g[8 * n : 8 * n + 8, LANES * i : LANES * i + LANES]
        part = load_pair(staged(fst, PLANES), u, lane)
        put(raw, [total[i] * part[i] for i in range(5)], u + 2)

    chunked(gather, 10)
    for i in range(2):
        put(raw, wrap_prev(get(raw, HALF + i), lane), i)
        put(raw, wrap_next(get(raw, 2 + i), lane), HALF + 2 + i)

    taps = filter_table()

    def smooth(u):
        part = [[], [], []]
        for i in range(5):
            r0 = raw[u + 2, i]
            r1 = raw[u + 1, i] + raw[u + 3, i]
            r2 = raw[u, i] + raw[u + 4, i]
            for b in range(3):
                part[b].append(float(taps[3, 3 + b]) * r0 + float(taps[4, 3 + b]) * r1 + float(taps[5, 3 + b]) * r2)
        acc = part[0]
        for b in (1, 2):
            up, down = next_lane(part[b], lane, b), prev_lane(part[b], lane, b)
            acc = [acc[i] + (up[i] + down[i]) for i in range(4)]
        store_pair(staged(stage, 6), u, acc)

    chunked(smooth, 10)
    stores += [
        pltpu.make_async_copy(stage.at[6, t, own], grad.at[:, pl.ds(LANES * t, LANES)], sems.at[2 + t]) for t in range(2)
    ]
    for copy in stores[2:]:
        copy.start()
    for copy in stores:
        copy.wait()


def advance(table, fields, inv_eps, fwd, mask, *edges):
    any_space = pl.BlockSpec(memory_space=pl.ANY)
    return pl.pallas_call(
        main_kernel,
        out_shape=(jax.ShapeDtypeStruct((6, T, T), f32), jax.ShapeDtypeStruct((T, T), f32)),
        in_specs=[pl.BlockSpec(memory_space=pltpu.SMEM)] + [any_space] * 10,
        out_specs=(any_space,) * 2,
        scratch_shapes=[
            pltpu.VMEM((7, 3, ROWS, LANES), f32),
            pltpu.VMEM((PLANES + 1, 3, ROWS, LANES), f32),
            pltpu.VMEM((T, T), jnp.int32),
            pltpu.VMEM((7, 64, LANES), f32),
            pltpu.VMEM((7, 64, LANES), f32),
            pltpu.VMEM((4, 32, LANES), f32),
            pltpu.VMEM((4, 32, LANES), f32),
            pltpu.VMEM((2 * STEPS * 4, 3 * K), bf16),
            pltpu.VMEM((STEPS + 1, 3, HALF, 5, 8, LANES), f32),
            pltpu.VMEM((3, HALF, 5, 8, LANES), f32),
            pltpu.VMEM((HALF, 5, 8, LANES), f32),
            pltpu.VMEM((HALF + 4, 5, 8, LANES), f32),
            pltpu.SemaphoreType.DMA((15,)),
        ],
        compiler_params=pltpu.CompilerParams(vmem_limit_bytes=48 * 2**20),
        name="advance",
    )(table, fields, inv_eps, fwd, mask, *edges)


def swap(x, axis, offset):
    count = lax.axis_size(axis)
    route = []
    for i in range(offset, count + offset, 2):
        a, b = i % count, (i + 1) % count
        route += [(a, b), (b, a)]
    return lax.ppermute(x, axis, route)


def coefficients(phase_start, omega):
    theta = phase_start[None] + omega[None] * jnp.arange(STEPS, dtype=f32)[:, None]
    table = jnp.stack([jnp.cos(theta), -jnp.sin(theta)], axis=2).reshape(STEPS, 2 * NF) / STEPS
    high = lax.reduce_precision(table, 8, 7)
    low = lax.reduce_precision(table - high, 8, 7)
    return jnp.concatenate([high, low, high], axis=1)


def local(fields, inv_eps, fwd_dft, phase_start, omega, mask):
    fwd = fwd_dft.reshape(PLANES, T, T)
    table = coefficients(phase_start, omega)
    xs0, xs1, ys0, ys1 = pack(fields, inv_eps, fwd, mask)
    y0 = swap(ys0, "gy", 0)
    y1 = swap(ys1, "gy", 1)
    x0 = swap(xs0, "gx", 0)
    x1 = swap(xs1, "gx", 1)
    even_x = lax.rem(lax.axis_index("gx"), 2) == 0
    even_y = lax.rem(lax.axis_index("gy"), 2) == 0
    right = jnp.where(even_y, y0, y1)
    left = jnp.where(even_y, y1, y0)
    lane = lax.broadcasted_iota(jnp.int32, (4, 32, LANES), 2)

    def corner(rows, group):
        r, l = right[:, rows], left[:, rows]
        r4, l4 = jnp.concatenate([r[4:], r[:1]]), jnp.concatenate([l[4:], l[:1]])
        block = lane // 32 * 32
        res = jnp.where(block == right_slot(group, 0), r[:4], l[:4])
        res = jnp.where(block == right_slot(group, 4), r4, res)
        return jnp.where(block == left_slot(group, 4), l4, res)

    up, down = corner(slice(32, 64), 3), corner(slice(0, 32), 0)
    c0 = swap(jnp.where(even_x, up, down), "gx", 0)
    c1 = swap(jnp.where(even_x, down, up), "gx", 1)
    return advance(table, fields, inv_eps, fwd, mask, y0, y1, x0, x1, c0, c1)


def solution(mesh):
    return jax.shard_map(
        local,
        mesh=mesh,
        in_specs=(
            P(None, "gx", "gy"),
            P("gx", "gy"),
            P(None, None, None, "gx", "gy"),
            P(),
            P(),
            P("gx", "gy"),
        ),
        out_specs=(P(None, "gx", "gy"), P("gx", "gy")),
        check_vma=False,
    )
```

time: 57.6 us -> 53.1 us (0.922)
  Pallas kernels: 34.6 us -> 30.5 us
  waiting for transfers between devices: 2.05 us -> 2.67 us
  local copies, waits for them, and re-layouts: 0.84 us -> 0.23 us
  other arithmetic: 0.93 us -> 0.34 us
    pallas_call x1, Pallas kernels: 29.1 us -> 25.8 us  [advance(): pl.pallas_call(main_kernel, out_shape=(jax.ShapeDtypeStruct((6, T, T), f3...]
    pallas_call x1, Pallas kernels: 5.5 us -> 4.73 us  [pack(): pl.pallas_call(pack_kernel, out_shape=(x_shape, x_shape, y_shape, y_shape...]
    ppermute x6, waiting for transfers between devices: 2.05 us -> 2.67 us  [swap(): return lax.ppermute(x, axis, route)]
    unnamed x16 -> x10, local copies, waits for them, and re-layouts: 0.64 us -> 0.03 us
    concatenate x1, other arithmetic: 0.67 us -> 0.08 us  [coefficients(): return jnp.concatenate([high, low, high], axis=1)]
  transfers between devices with their start and end apart: 6 -> 6, of which waited for: 2 -> 2; matrix products, arithmetic and copies ran while one was open for 2% -> 1% of each run, Pallas kernels for 0% -> 0%
where the time goes in v3:
time: 53.1 us; the launch traced here: 53 us
  Pallas kernels  30.5 us (57%)
  starting transfers between devices  18.3 us (34%)
  waiting for transfers between devices  2.67 us (5%)
  between operations  0.95 us (2%)
    pallas_call x1, Pallas kernels, advance(): pl.pallas_call(main_kernel, out_shape=(jax.ShapeDtypeStruct((6, T, T), f3...  25.8 us
    ppermute x6, starting transfers between devices, swap(): return lax.ppermute(x, axis, route)  18.3 us
    pallas_call x1, Pallas kernels, pack(): pl.pallas_call(pack_kernel, out_shape=(x_shape, x_shape, y_shape, y_shape...  4.73 us
    ppermute x6, waiting for transfers between devices, swap(): return lax.ppermute(x, axis, route)  2.67 us
  transfers between devices with their start and end apart: 6, of which 2 were waited for; matrix products, arithmetic and copies ran while one was open for 1% of the time, Pallas kernels for 0%

profile of v3, /device:TPU:16, one launch (start us, length us, event | category | flops | bytes accessed | tf_op | source)
XLA Modules:
  0.0 53.0 jit_solution(6906781936604706830)
XLA Ops:
  0.6 0.0 copy-start.3
  0.6 0.0 copy-start.4
  0.6 4.7 %pack.1 = (f32[7,32,256]{2,1,0:T(8,128)}, f32[7,32,256]{2,1,0:T(8,128)}, f32[7,64,128]{2,1,0:T(8,128)}, f32[7,64,128]{2,1,0:T(8,128)}) custom-call(f32[6,256,256]{2,1,0:T(8,128)} %fields.3, f32[256,256]{1,0:T(8,128)} %inv_eps.3, f32[18,256,256]{2,1,0:T(8,128)} %bitcast.3, s32[256,256]{1,0:T(8,128)} %mask.3), custom_call_target="tpu_custom_call" | custom-call | flops 10000000 | bytes 7000000 | tf_op jit(solution)/shard_map/pack/pallas_call | solution.py:144
  5.4 0.0 copy-start
  5.4 0.0 copy-start.1
  5.4 0.0 copy-start.2
  5.4 0.1 collective-permute-start
  5.5 2.6 %collective-permute-start.1 = (f32[7,64,128]{2,1,0:T(8,128)}, f32[7,64,128]{2,1,0:T(8,128)S(1)}, u32[]{:S(2)}, u32[]{:S(2)}) collective-permute-start(f32[7,64,128]{2,1,0:T(8,128)} %get-tuple-element.7), channel_id=1, source_target_pairs={{1,2},{2,1},{3,4},{4,3},{5,6},{6,5},{7,8},{8,7},{9,10},{10,9},{11,... | collective-permute-start | bytes 688136 | tf_op jit(solution)/shard_map/ppermute | solution.py:479
  8.2 2.2 %collective-permute-start.2 = (f32[7,32,256]{2,1,0:T(8,128)}, f32[7,32,256]{2,1,0:T(8,128)S(1)}, u32[]{:S(2)}, u32[]{:S(2)}) collective-permute-start(f32[7,32,256]{2,1,0:T(8,128)} %get-tuple-element.8), channel_id=1, source_target_pairs={{0,16},{16,0},{32,48},{48,32},{64,80},{80,64},{96,112},{112,96},{1... | collective-permute-start | bytes 688136 | tf_op jit(solution)/shard_map/ppermute | solution.py:479
  10.3 5.3 %collective-permute-start.3 = (f32[7,32,256]{2,1,0:T(8,128)}, f32[7,32,256]{2,1,0:T(8,128)S(1)}, u32[]{:S(2)}, u32[]{:S(2)}) collective-permute-start(f32[7,32,256]{2,1,0:T(8,128)} %get-tuple-element.9), channel_id=1, source_target_pairs={{16,32},{32,16},{48,64},{64,48},{80,96},{96,80},{112,128},{128,112... | collective-permute-start | bytes 688136 | tf_op jit(solution)/shard_map/ppermute | solution.py:479
  15.6 0.0 copy-done.3
  15.6 0.0 copy-done.4
  15.7 0.1 fusion.8
  15.8 0.1 copy.10
  15.9 0.1 copy.12
  16.0 0.0 collective-permute-done.y0
  16.0 0.5 collective-permute-done.1.y1
  16.7 0.1 collective-permute-start.4
  16.8 8.0 %collective-permute-start.5 = (f32[4,32,128]{2,1,0:T(8,128)S(1)}, f32[4,32,128]{2,1,0:T(8,128)S(1)}, u32[]{:S(2)}, u32[]{:S(2)}) collective-permute-start(f32[4,32,128]{2,1,0:T(8,128)S(1)} %get-tuple-element.10), channel_id=1, source_target_pairs={{16,32},{32,16},{48,64},{64,48},{80,96},{96,80},{112,128},{128,112... | collective-permute-start | bytes 196616 | tf_op jit(solution)/shard_map/ppermute | solution.py:479
  24.8 0.1 pad_maximum_fusion.table
  24.8 0.0 collective-permute-done.2.x0
  24.8 0.0 collective-permute-done.3.x1
  24.9 0.0 collective-permute-done.4.c0
  24.9 2.1 %collective-permute-done.5.c1 = f32[4,32,128]{2,1,0:T(8,128)S(1)} collective-permute-done((f32[4,32,128]{2,1,0:T(8,128)S(1)}, f32[4,32,128]{2,1,0:T(8,128)S(1)}, u32[]{:S(2)}, u32[]{:S(2)}) %collective-permute-start.5) | collective-permute-done | bytes 65568 | tf_op jit(solution)/shard_map/ppermute | solution.py:479
  27.0 0.0 copy-done
  27.0 0.0 copy-done.1
  27.0 0.0 copy-done.2
  27.0 25.8 %advance.1 = (f32[6,256,256]{2,1,0:T(8,128)}, f32[256,256]{1,0:T(8,128)}) custom-call(f32[24,18]{1,0:T(8,128)S(1)} %pad_maximum_fusion.table, f32[6,256,256]{2,1,0:T(8,128)S(1)} %copy-done, f32[256,256]{1,0:T(8,128)S(1)} %copy-done.1, f32[18,256,256]{2,1,0:T(8,128)} %bitcast.4, s32[256,256]{1,0:T(8,128)S(1)} %copy-done.2, ...), custom_call_target="tpu_custom_call" | custom-call | tf_op jit(solution)/shard_map/advance/pallas_call | solution.py:448
  (11 shorter events, 0.2 us)
Async XLA Ops:
  0.6 15.0 %copy-start.3 = (f32[3]{0:T(128)S(1)}, f32[3]{0:T(128)}, u32[]{:S(2)}) copy-start(f32[3]{0:T(128)} %param.10) | copy-start | bytes 40
  0.6 15.0 %copy-start.4 = (f32[3]{0:T(128)S(1)}, f32[3]{0:T(128)}, u32[]{:S(2)}) copy-start(f32[3]{0:T(128)} %param.9) | copy-start | bytes 40
  5.4 21.6 %copy-start = (f32[6,256,256]{2,1,0:T(8,128)S(1)}, f32[6,256,256]{2,1,0:T(8,128)}, u32[]{:S(2)}) copy-start(f32[6,256,256]{2,1,0:T(8,128)} %fields.3) | copy-start | bytes 4718596
  5.4 21.6 %copy-start.1 = (f32[256,256]{1,0:T(8,128)S(1)}, f32[256,256]{1,0:T(8,128)}, u32[]{:S(2)}) copy-start(f32[256,256]{1,0:T(8,128)} %inv_eps.3) | copy-start | bytes 786436
  5.4 21.6 %copy-start.2 = (s32[256,256]{1,0:T(8,128)S(1)}, s32[256,256]{1,0:T(8,128)}, u32[]{:S(2)}) copy-start(s32[256,256]{1,0:T(8,128)} %mask.3) | copy-start | bytes 786436
  5.4 10.6 %collective-permute-start = (f32[7,64,128]{2,1,0:T(8,128)}, f32[7,64,128]{2,1,0:T(8,128)S(1)}, u32[]{:S(2)}, u32[]{:S(2)}) collective-permute-start(f32[7,64,128]{2,1,0:T(8,128)} %get-tuple-element.6), channel_id=1, source_target_pairs={{0,1},{1,0},{2,3},{3,2},{4,5},{5,4},{6,7},{7,6},{8,9},{9,8},{10,11... | collective-permute-start | bytes 688136 | tf_op jit(solution)/shard_map/ppermute | solution.py:479
  5.5 11.0 %collective-permute-start.1 = (f32[7,64,128]{2,1,0:T(8,128)}, f32[7,64,128]{2,1,0:T(8,128)S(1)}, u32[]{:S(2)}, u32[]{:S(2)}) collective-permute-start(f32[7,64,128]{2,1,0:T(8,128)} %get-tuple-element.7), channel_id=1, source_target_pairs={{1,2},{2,1},{3,4},{4,3},{5,6},{6,5},{7,8},{8,7},{9,10},{10,9},{11,... | collective-permute-start | bytes 688136 | tf_op jit(solution)/shard_map/ppermute | solution.py:479
  8.2 16.7 %collective-permute-start.2 = (f32[7,32,256]{2,1,0:T(8,128)}, f32[7,32,256]{2,1,0:T(8,128)S(1)}, u32[]{:S(2)}, u32[]{:S(2)}) collective-permute-start(f32[7,32,256]{2,1,0:T(8,128)} %get-tuple-element.8), channel_id=1, source_target_pairs={{0,16},{16,0},{32,48},{48,32},{64,80},{80,64},{96,112},{112,96},{1... | collective-permute-start | bytes 688136 | tf_op jit(solution)/shard_map/ppermute | solution.py:479
  10.3 14.5 %collective-permute-start.3 = (f32[7,32,256]{2,1,0:T(8,128)}, f32[7,32,256]{2,1,0:T(8,128)S(1)}, u32[]{:S(2)}, u32[]{:S(2)}) collective-permute-start(f32[7,32,256]{2,1,0:T(8,128)} %get-tuple-element.9), channel_id=1, source_target_pairs={{16,32},{32,16},{48,64},{64,48},{80,96},{96,80},{112,128},{128,112... | collective-permute-start | bytes 688136 | tf_op jit(solution)/shard_map/ppermute | solution.py:479
  16.7 8.2 %collective-permute-start.4 = (f32[4,32,128]{2,1,0:T(8,128)S(1)}, f32[4,32,128]{2,1,0:T(8,128)S(1)}, u32[]{:S(2)}, u32[]{:S(2)}) collective-permute-start(f32[4,32,128]{2,1,0:T(8,128)S(1)} %broadcast_select_fusion.3), channel_id=1, source_target_pairs={{0,16},{16,0},{32,48},{48,32},{64,80},{80,64},{96,112},{112,96},{1... | collective-permute-start | bytes 196616 | tf_op jit(solution)/shard_map/ppermute | solution.py:479
  16.8 10.2 %collective-permute-start.5 = (f32[4,32,128]{2,1,0:T(8,128)S(1)}, f32[4,32,128]{2,1,0:T(8,128)S(1)}, u32[]{:S(2)}, u32[]{:S(2)}) collective-permute-start(f32[4,32,128]{2,1,0:T(8,128)S(1)} %get-tuple-element.10), channel_id=1, source_target_pairs={{16,32},{32,16},{48,64},{64,48},{80,96},{96,80},{112,128},{128,112... | collective-permute-start | bytes 196616 | tf_op jit(solution)/shard_map/ppermute | solution.py:479

commit v4 on v3

--- a/solution.py
+++ b/solution.py
@@ -78,29 +78,28 @@
 def pack_kernel(fields, inv_eps, fwd, mask, xs0, xs1, ys0, ys1, f7, fw, mk, sems):
     even_x = lax.rem(lax.axis_index("gx"), 2) == 0
     even_y = lax.rem(lax.axis_index("gy"), 2) == 0
-    loads = [
-        pltpu.make_async_copy(fields, f7.at[pl.ds(0, 6)], sems.at[0]),
-        pltpu.make_async_copy(inv_eps, f7.at[6], sems.at[1]),
-        pltpu.make_async_copy(mask, mk, sems.at[2]),
-    ]
-    loads += [
-        pltpu.make_async_copy(fwd.at[pl.ds(3 * k, 3)], fw.at[pl.ds(3 * k, 3)], sems.at[3 + k]) for k in range(6)
-    ]
-    for copy in loads:
-        copy.start()
+    loads = [[
+        pltpu.make_async_copy(inv_eps, f7.at[6], sems.at[0]),
+        pltpu.make_async_copy(mask, mk, sems.at[1]),
+    ]]
+    for k in range(6):
+        loads.append([
+            pltpu.make_async_copy(fields.at[k], f7.at[k], sems.at[2 + k]),
+            pltpu.make_async_copy(fwd.at[pl.ds(3 * k, 3)], fw.at[pl.ds(3 * k, 3)], sems.at[8 + k]),
+        ])
+    for piece in loads:
+        for copy in piece:
+            copy.start()
     lane = lane_iota()
 
     def rows(ref, k, g, j, t):
         return ref[k, pl.ds(64 * g + 8 * j, 8), pl.ds(LANES * t, LANES)]
 
-    loads[0].wait()
-    loads[1].wait()
-    for k in (6, 0, 1, 2, 3, 4, 5):
+    for k, piece in zip((6, 0, 1, 2, 3, 4, 5), loads, strict=True):
+        for copy in piece:
+            copy.wait()
         if k == 6:
-            loads[2].wait()
             fw[PLANES] = mk[...].astype(f32)
-        else:
-            loads[3 + k].wait()
         for j in range(8):
             first = last = None
             for g in range(4):
@@ -150,7 +149,7 @@
             pltpu.VMEM((7, T, T), f32),
             pltpu.VMEM((PLANES + 1, T, T), f32),
             pltpu.VMEM((T, T), jnp.int32),
-            pltpu.SemaphoreType.DMA((9,)),
+            pltpu.SemaphoreType.DMA((14,)),
         ],
         compiler_params=pltpu.CompilerParams(vmem_limit_bytes=56 * 2**20),
         cost_estimate=pl.CostEstimate(flops=10**7, bytes_accessed=7 * 10**6, transcendentals=0),
@@ -270,12 +269,12 @@
     sub = lax.broadcasted_iota(jnp.int32, (8, LANES), 0)
     right_half = lane < 64
 
-    def fill(j, _):
-        at = pl.ds(pl.multiple_of(8 * j, 8), 8)
+    def fill(j):
+        at = pl.ds(8 * j, 8)
         for k in range(7):
             r, l = yr[k, at], yl[k, at]
             for g in range(4):
-                to = pl.ds(pl.multiple_of(PAD + 64 * g + 8 * j, 8), 8)
+                to = pl.ds(PAD + 64 * g + 8 * j, 8)
                 stage[k, 2, to] = jnp.where(
                     right_half, turn(r, -right_slot(g, k), 1), turn(l, 96 - left_slot(g, k), 1)
                 )
@@ -285,9 +284,9 @@
                         turn(r, -right_slot(g, k) - 26 - 2 * jj, 1),
                         turn(l, 126 - left_slot(g, k) - 2 * jj, 1),
                     )
-        return 0
-
-    lax.fori_loop(0, 8, fill, 0)
+
+    for j in range(8):
+        fill(j)
     zero = jnp.zeros((8, LANES), f32)
     for k in range(7):
         c = k % 4

time: 53.1 us -> 52.2 us (0.983)
  Pallas kernels: 30.5 us -> 29.7 us
where the time goes in v4:
time: 52.2 us; the launch traced here: 52.1 us
  Pallas kernels  29.7 us (57%)
  starting transfers between devices  18.3 us (35%)
  waiting for transfers between devices  2.67 us (5%)
  between operations  0.95 us (2%)
    pallas_call x1, Pallas kernels, advance(): pl.pallas_call(main_kernel, out_shape=(jax.ShapeDtypeStruct((6, T, T), f3...  25.3 us
    ppermute x6, starting transfers between devices, swap(): return lax.ppermute(x, axis, route)  18.3 us
    pallas_call x1, Pallas kernels, pack(): pl.pallas_call(pack_kernel, out_shape=(x_shape, x_shape, y_shape, y_shape...  4.39 us
    ppermute x6, waiting for transfers between devices, swap(): return lax.ppermute(x, axis, route)  2.67 us
  transfers between devices with their start and end apart: 6, of which 2 were waited for; matrix products, arithmetic and copies ran while one was open for 1% of the time, Pallas kernels for 0%

profile of v4, /device:TPU:16, one launch (start us, length us, event | category | flops | bytes accessed | tf_op | source)
XLA Modules:
  0.0 52.1 jit_solution(5159279719760736522)
XLA Ops:
  0.6 0.0 copy-start.3
  0.6 0.0 copy-start.4
  0.6 4.4 %pack.1 = (f32[7,32,256]{2,1,0:T(8,128)}, f32[7,32,256]{2,1,0:T(8,128)}, f32[7,64,128]{2,1,0:T(8,128)}, f32[7,64,128]{2,1,0:T(8,128)}) custom-call(f32[6,256,256]{2,1,0:T(8,128)} %fields.3, f32[256,256]{1,0:T(8,128)} %inv_eps.3, f32[18,256,256]{2,1,0:T(8,128)} %bitcast.3, s32[256,256]{1,0:T(8,128)} %mask.3), custom_call_target="tpu_custom_call" | custom-call | flops 10000000 | bytes 7000000 | tf_op jit(solution)/shard_map/pack/pallas_call | solution.py:143
  5.1 0.0 copy-start
  5.1 0.0 copy-start.1
  5.1 0.0 copy-start.2
  5.1 0.1 collective-permute-start
  5.2 2.6 %collective-permute-start.1 = (f32[7,64,128]{2,1,0:T(8,128)}, f32[7,64,128]{2,1,0:T(8,128)S(1)}, u32[]{:S(2)}, u32[]{:S(2)}) collective-permute-start(f32[7,64,128]{2,1,0:T(8,128)} %get-tuple-element.7), channel_id=1, source_target_pairs={{1,2},{2,1},{3,4},{4,3},{5,6},{6,5},{7,8},{8,7},{9,10},{10,9},{11,... | collective-permute-start | bytes 688136 | tf_op jit(solution)/shard_map/ppermute | solution.py:478
  7.8 2.2 %collective-permute-start.2 = (f32[7,32,256]{2,1,0:T(8,128)}, f32[7,32,256]{2,1,0:T(8,128)S(1)}, u32[]{:S(2)}, u32[]{:S(2)}) collective-permute-start(f32[7,32,256]{2,1,0:T(8,128)} %get-tuple-element.8), channel_id=1, source_target_pairs={{0,16},{16,0},{32,48},{48,32},{64,80},{80,64},{96,112},{112,96},{1... | collective-permute-start | bytes 688136 | tf_op jit(solution)/shard_map/ppermute | solution.py:478
  10.0 5.3 %collective-permute-start.3 = (f32[7,32,256]{2,1,0:T(8,128)}, f32[7,32,256]{2,1,0:T(8,128)S(1)}, u32[]{:S(2)}, u32[]{:S(2)}) collective-permute-start(f32[7,32,256]{2,1,0:T(8,128)} %get-tuple-element.9), channel_id=1, source_target_pairs={{16,32},{32,16},{48,64},{64,48},{80,96},{96,80},{112,128},{128,112... | collective-permute-start | bytes 688136 | tf_op jit(solution)/shard_map/ppermute | solution.py:478
  15.3 0.0 copy-done.3
  15.3 0.0 copy-done.4
  15.3 0.1 fusion.8
  15.5 0.1 copy.10
  15.6 0.1 copy.12
  15.7 0.0 collective-permute-done.y0
  15.7 0.5 collective-permute-done.1.y1
  16.4 0.1 collective-permute-start.4
  16.5 8.0 %collective-permute-start.5 = (f32[4,32,128]{2,1,0:T(8,128)S(1)}, f32[4,32,128]{2,1,0:T(8,128)S(1)}, u32[]{:S(2)}, u32[]{:S(2)}) collective-permute-start(f32[4,32,128]{2,1,0:T(8,128)S(1)} %get-tuple-element.10), channel_id=1, source_target_pairs={{16,32},{32,16},{48,64},{64,48},{80,96},{96,80},{112,128},{128,112... | collective-permute-start | bytes 196616 | tf_op jit(solution)/shard_map/ppermute | solution.py:478
  24.4 0.1 pad_maximum_fusion.table
  24.5 0.0 collective-permute-done.2.x0
  24.5 0.0 collective-permute-done.3.x1
  24.5 0.0 collective-permute-done.4.c0
  24.5 2.1 %collective-permute-done.5.c1 = f32[4,32,128]{2,1,0:T(8,128)S(1)} collective-permute-done((f32[4,32,128]{2,1,0:T(8,128)S(1)}, f32[4,32,128]{2,1,0:T(8,128)S(1)}, u32[]{:S(2)}, u32[]{:S(2)}) %collective-permute-start.5) | collective-permute-done | bytes 65568 | tf_op jit(solution)/shard_map/ppermute | solution.py:478
  26.7 0.0 copy-done
  26.7 0.0 copy-done.1
  26.7 0.0 copy-done.2
  26.7 25.3 %advance.1 = (f32[6,256,256]{2,1,0:T(8,128)}, f32[256,256]{1,0:T(8,128)}) custom-call(f32[24,18]{1,0:T(8,128)S(1)} %pad_maximum_fusion.table, f32[6,256,256]{2,1,0:T(8,128)S(1)} %copy-done, f32[256,256]{1,0:T(8,128)S(1)} %copy-done.1, f32[18,256,256]{2,1,0:T(8,128)} %bitcast.4, s32[256,256]{1,0:T(8,128)S(1)} %copy-done.2, ...), custom_call_target="tpu_custom_call" | custom-call | tf_op jit(solution)/shard_map/advance/pallas_call | solution.py:447
  (11 shorter events, 0.2 us)
Async XLA Ops:
  0.6 14.7 %copy-start.3 = (f32[3]{0:T(128)S(1)}, f32[3]{0:T(128)}, u32[]{:S(2)}) copy-start(f32[3]{0:T(128)} %param.10) | copy-start | bytes 40
  0.6 14.7 %copy-start.4 = (f32[3]{0:T(128)S(1)}, f32[3]{0:T(128)}, u32[]{:S(2)}) copy-start(f32[3]{0:T(128)} %param.9) | copy-start | bytes 40
  5.1 21.6 %copy-start = (f32[6,256,256]{2,1,0:T(8,128)S(1)}, f32[6,256,256]{2,1,0:T(8,128)}, u32[]{:S(2)}) copy-start(f32[6,256,256]{2,1,0:T(8,128)} %fields.3) | copy-start | bytes 4718596
  5.1 21.6 %copy-start.1 = (f32[256,256]{1,0:T(8,128)S(1)}, f32[256,256]{1,0:T(8,128)}, u32[]{:S(2)}) copy-start(f32[256,256]{1,0:T(8,128)} %inv_eps.3) | copy-start | bytes 786436
  5.1 21.6 %copy-start.2 = (s32[256,256]{1,0:T(8,128)S(1)}, s32[256,256]{1,0:T(8,128)}, u32[]{:S(2)}) copy-start(s32[256,256]{1,0:T(8,128)} %mask.3) | copy-start | bytes 786436
  5.1 10.6 %collective-permute-start = (f32[7,64,128]{2,1,0:T(8,128)}, f32[7,64,128]{2,1,0:T(8,128)S(1)}, u32[]{:S(2)}, u32[]{:S(2)}) collective-permute-start(f32[7,64,128]{2,1,0:T(8,128)} %get-tuple-element.6), channel_id=1, source_target_pairs={{0,1},{1,0},{2,3},{3,2},{4,5},{5,4},{6,7},{7,6},{8,9},{9,8},{10,11... | collective-permute-start | bytes 688136 | tf_op jit(solution)/shard_map/ppermute | solution.py:478
  5.2 11.0 %collective-permute-start.1 = (f32[7,64,128]{2,1,0:T(8,128)}, f32[7,64,128]{2,1,0:T(8,128)S(1)}, u32[]{:S(2)}, u32[]{:S(2)}) collective-permute-start(f32[7,64,128]{2,1,0:T(8,128)} %get-tuple-element.7), channel_id=1, source_target_pairs={{1,2},{2,1},{3,4},{4,3},{5,6},{6,5},{7,8},{8,7},{9,10},{10,9},{11,... | collective-permute-start | bytes 688136 | tf_op jit(solution)/shard_map/ppermute | solution.py:478
  7.8 16.7 %collective-permute-start.2 = (f32[7,32,256]{2,1,0:T(8,128)}, f32[7,32,256]{2,1,0:T(8,128)S(1)}, u32[]{:S(2)}, u32[]{:S(2)}) collective-permute-start(f32[7,32,256]{2,1,0:T(8,128)} %get-tuple-element.8), channel_id=1, source_target_pairs={{0,16},{16,0},{32,48},{48,32},{64,80},{80,64},{96,112},{112,96},{1... | collective-permute-start | bytes 688136 | tf_op jit(solution)/shard_map/ppermute | solution.py:478
  10.0 14.5 %collective-permute-start.3 = (f32[7,32,256]{2,1,0:T(8,128)}, f32[7,32,256]{2,1,0:T(8,128)S(1)}, u32[]{:S(2)}, u32[]{:S(2)}) collective-permute-start(f32[7,32,256]{2,1,0:T(8,128)} %get-tuple-element.9), channel_id=1, source_target_pairs={{16,32},{32,16},{48,64},{64,48},{80,96},{96,80},{112,128},{128,112... | collective-permute-start | bytes 688136 | tf_op jit(solution)/shard_map/ppermute | solution.py:478
  16.4 8.2 %collective-permute-start.4 = (f32[4,32,128]{2,1,0:T(8,128)S(1)}, f32[4,32,128]{2,1,0:T(8,128)S(1)}, u32[]{:S(2)}, u32[]{:S(2)}) collective-permute-start(f32[4,32,128]{2,1,0:T(8,128)S(1)} %broadcast_select_fusion.3), channel_id=1, source_target_pairs={{0,16},{16,0},{32,48},{48,32},{64,80},{80,64},{96,112},{112,96},{1... | collective-permute-start | bytes 196616 | tf_op jit(solution)/shard_map/ppermute | solution.py:478
  16.5 10.2 %collective-permute-start.5 = (f32[4,32,128]{2,1,0:T(8,128)S(1)}, f32[4,32,128]{2,1,0:T(8,128)S(1)}, u32[]{:S(2)}, u32[]{:S(2)}) collective-permute-start(f32[4,32,128]{2,1,0:T(8,128)S(1)} %get-tuple-element.10), channel_id=1, source_target_pairs={{16,32},{32,16},{48,64},{64,48},{80,96},{96,80},{112,128},{128,112... | collective-permute-start | bytes 196616 | tf_op jit(solution)/shard_map/ppermute | solution.py:478
